TPU v7x, 32 devices: a whole 2x2x4 slice. The times are simulated.
32 devices in a mesh: section: 2 (over y), dp: 16 (over z, x, core).
Axes of the slice: x: 2, y: 2, z: 4, core: 2. Of those that a mesh axis runs over, the one named last changes fastest.
Arguments:
- block_input: bfloat16 [65536, 256], P('dp'), may hold values from -6 to 6
- embedding: bfloat16 [65536, 256], P('dp'), may hold values from -6 to 6
- out_grad: bfloat16 [65536, 256], P('dp'), may hold values from -6 to 6
- example_counts: int32 [512], P('dp'), may hold values from 10 to 50
- example_lengths: int32 [512, 50], P('dp'), may hold values from 1 to 2
- norm1_gain: bfloat16 [256], replicated, may hold values from 0.25 to 1.75
- norm1_bias: bfloat16 [256], replicated, may hold values from -1.5 to 1.5
- query_weight: bfloat16 [256, 256], replicated, may hold values from -0.375 to 0.375
- query_bias: bfloat16 [256], replicated, may hold values from -1.5 to 1.5
- key_weight: bfloat16 [256, 256], replicated, may hold values from -0.375 to 0.375
- value_weight: bfloat16 [256, 256], replicated, may hold values from -0.375 to 0.375
- value_bias: bfloat16 [256], replicated, may hold values from -1.5 to 1.5
- out_weight: bfloat16 [256, 256], replicated, may hold values from -1 to 1
- out_bias: bfloat16 [256], replicated, may hold values from -1.5 to 1.5
- norm2_gain: bfloat16 [256], replicated, may hold values from 0.25 to 1.75
- norm2_bias: bfloat16 [256], replicated, may hold values from -1.5 to 1.5
- up_weight: bfloat16 [256, 1024], replicated, may hold values from -0.375 to 0.375
- up_bias: bfloat16 [1024], replicated, may hold values from -1.5 to 1.5
- down_weight: bfloat16 [1024, 256], replicated, may hold values from -0.1875 to 0.1875
- down_bias: bfloat16 [256], replicated, may hold values from -1.5 to 1.5
Outputs:
- states: bfloat16 [2, 65536, 256], P('section', 'dp')
- state_grads: float32 [2, 65536, 256], P('section', 'dp')
- grad_norm1_gain: float32 [256], replicated
- grad_norm1_bias: float32 [256], replicated
- grad_query_weight: float32 [256, 256], replicated
- grad_query_bias: float32 [256], replicated
- grad_key_weight: float32 [256, 256], replicated
- grad_value_weight: float32 [256, 256], replicated
- grad_value_bias: float32 [256], replicated
- grad_out_weight: float32 [256, 256], replicated
- grad_out_bias: float32 [256], replicated
- grad_norm2_gain: float32 [256], replicated
- grad_norm2_bias: float32 [256], replicated
- grad_up_weight: float32 [256, 1024], replicated
- grad_up_bias: float32 [1024], replicated
- grad_down_weight: float32 [1024, 256], replicated
- grad_down_bias: float32 [256], replicated
Inputs may be any that keep to these rules, and one draw needn't show every extreme that they name: Prompt p uses its first sum of example_lengths[p, j] over j < example_counts[p] slots, at most 100.
All inputs are finite; a program needn't handle non-finite values.
Results may differ from a plain program's by a relative error of at most 0.013.
Values may be sent and summed in bfloat16 or wider, within the bound.
A program may use at most 128 MiB of HBM per device.

v0:
```python
import jax
import jax.numpy as jnp
from jax import lax
from jax.sharding import PartitionSpec as P

HEADS = 8
SLOTS = 128
PER_ROW = 8
MAXEX = 50


def passed_along(block, axis, distance):
    devices = range(lax.axis_size(axis))
    route = [(i - distance, i) for i in devices if i - distance in devices]
    return lax.ppermute(block, axis, route)


def norm_parts(values_in, ln_gain, ln_shift):
    row_mean = jnp.mean(values_in, axis=-1, keepdims=True)
    centred = values_in - row_mean
    spread = jnp.mean(centred * centred, axis=-1, keepdims=True)
    inverse = lax.rsqrt(spread + 1e-05)
    unit_rows = centred * inverse
    return (unit_rows * ln_gain + ln_shift, unit_rows, inverse)


def norm_back(grad_out, unit_rows, inverse, ln_gain):
    scaled = grad_out * ln_gain
    scaled_mean = jnp.mean(scaled, axis=-1, keepdims=True)
    cross_mean = jnp.mean(scaled * unit_rows, axis=-1, keepdims=True)
    grad_in = inverse * (scaled - scaled_mean - unit_rows * cross_mean)
    return (grad_in, jnp.sum(grad_out * unit_rows, axis=0), jnp.sum(grad_out, axis=0))


def matmul(left_op, right_op):
    return jnp.dot(left_op, right_op, preferred_element_type=jnp.float32)


def matmul_tn(left_op, right_op):
    return lax.dot_general(
        left_op, right_op, (((0,), (0,)), ((), ())), preferred_element_type=jnp.float32
    )


def matmul_nt(left_op, right_op):
    return lax.dot_general(
        left_op, right_op, (((1,), (1,)), ((), ())), preferred_element_type=jnp.float32
    )


def column_sum(grad_low):
    return jnp.sum(grad_low.astype(jnp.float32), axis=0)


def forward_parts(stream, keep_mask, params):
    (
        norm1_gain,
        norm1_bias,
        query_weight,
        query_bias,
        key_weight,
        value_weight,
        value_bias,
        out_weight,
        out_bias,
        norm2_gain,
        norm2_bias,
        up_weight,
        up_bias,
        down_weight,
        down_bias,
    ) = params
    row_count, model_width = stream.shape
    prompt_count = keep_mask.shape[0]
    slot_count = keep_mask.shape[1]
    head_size = model_width // HEADS
    score_scale = head_size ** (-0.5)
    normed_one, unit_one, inverse_one = norm_parts(
        stream, norm1_gain.astype(jnp.float32), norm1_bias.astype(jnp.float32)
    )
    normed_one = normed_one.astype(jnp.bfloat16)
    query_low = (matmul(normed_one, query_weight) + query_bias.astype(jnp.float32)).astype(
        jnp.bfloat16
    )
    key_low = matmul(normed_one, key_weight).astype(jnp.bfloat16)
    value_low = (matmul(normed_one, value_weight) + value_bias.astype(jnp.float32)).astype(
        jnp.bfloat16
    )
    query_heads = query_low.reshape(prompt_count, slot_count, HEADS, head_size)
    key_heads = key_low.reshape(prompt_count, slot_count, HEADS, head_size)
    value_heads = value_low.reshape(prompt_count, slot_count, HEADS, head_size)
    scores = (
        jnp.einsum("pqhd,pkhd->phqk", query_heads, key_heads, preferred_element_type=jnp.float32)
        * score_scale
    )
    scores = jnp.where(keep_mask[:, None], scores, -1e30)
    row_max = jnp.max(scores, axis=-1, keepdims=True)
    shifted = jnp.exp(scores - row_max)
    probabilities = shifted / jnp.sum(shifted, axis=-1, keepdims=True)
    weights_low = probabilities.astype(jnp.bfloat16)
    mixed_low = jnp.einsum(
        "phqk,pkhd->pqhd", weights_low, value_heads, preferred_element_type=jnp.float32
    )
    mixed_low = mixed_low.reshape(row_count, model_width).astype(jnp.bfloat16)
    middle = stream + matmul(mixed_low, out_weight) + out_bias.astype(jnp.float32)
    normed_two, unit_two, inverse_two = norm_parts(
        middle, norm2_gain.astype(jnp.float32), norm2_bias.astype(jnp.float32)
    )
    normed_two = normed_two.astype(jnp.bfloat16)
    pre_gelu = matmul(normed_two, up_weight) + up_bias.astype(jnp.float32)
    hidden = jax.nn.gelu(pre_gelu).astype(jnp.bfloat16)
    result = middle + matmul(hidden, down_weight) + down_bias.astype(jnp.float32)
    saved_parts = (
        normed_one,
        unit_one,
        inverse_one,
        query_heads,
        key_heads,
        value_heads,
        probabilities,
        weights_low,
        mixed_low,
        unit_two,
        inverse_two,
        normed_two,
        pre_gelu,
        hidden,
    )
    return (result, saved_parts)


def backward_parts(stream, keep_mask, grad_result, params):
    (
        norm1_gain,
        norm1_bias,
        query_weight,
        query_bias,
        key_weight,
        value_weight,
        value_bias,
        out_weight,
        out_bias,
        norm2_gain,
        norm2_bias,
        up_weight,
        up_bias,
        down_weight,
        down_bias,
    ) = params
    result, saved_parts = forward_parts(stream, keep_mask, params)
    (
        normed_one,
        unit_one,
        inverse_one,
        query_heads,
        key_heads,
        value_heads,
        probabilities,
        weights_low,
        mixed_low,
        unit_two,
        inverse_two,
        normed_two,
        pre_gelu,
        hidden,
    ) = saved_parts
    row_count, model_width = stream.shape
    prompt_count, slot_count, head_count, head_size = query_heads.shape
    score_scale = head_size ** (-0.5)
    out_low = grad_result.astype(jnp.bfloat16)
    grad_down_weight = matmul_tn(hidden, out_low)
    grad_down_bias = column_sum(out_low)
    grad_hidden = matmul_nt(out_low, down_weight)
    _, gelu_pull = jax.vjp(jax.nn.gelu, pre_gelu)
    grad_pre = gelu_pull(grad_hidden)[0].astype(jnp.bfloat16)
    grad_up_weight = matmul_tn(normed_two, grad_pre)
    grad_up_bias = column_sum(grad_pre)
    grad_normed_two = matmul_nt(grad_pre, up_weight)
    grad_from_two, grad_norm2_gain, grad_norm2_bias = norm_back(
        grad_normed_two, unit_two, inverse_two, norm2_gain.astype(jnp.float32)
    )
    grad_middle = grad_result + grad_from_two
    attn_low = grad_middle.astype(jnp.bfloat16)
    grad_out_weight = matmul_tn(mixed_low, attn_low)
    grad_out_bias = column_sum(attn_low)
    grad_mixed = matmul_nt(attn_low, out_weight).astype(jnp.bfloat16)
    grad_mixed = grad_mixed.reshape(prompt_count, slot_count, head_count, head_size)
    grad_values = jnp.einsum(
        "phqk,pqhd->pkhd", weights_low, grad_mixed, preferred_element_type=jnp.float32
    )
    grad_values = grad_values.reshape(row_count, model_width).astype(jnp.bfloat16)
    grad_probs = jnp.einsum(
        "pqhd,pkhd->phqk", grad_mixed, value_heads, preferred_element_type=jnp.float32
    )
    grad_scores = probabilities * (
        grad_probs - jnp.sum(probabilities * grad_probs, axis=-1, keepdims=True)
    )
    grad_scores = grad_scores.astype(jnp.bfloat16)
    grad_queries = (
        jnp.einsum("phqk,pkhd->pqhd", grad_scores, key_heads, preferred_element_type=jnp.float32)
        * score_scale
    )
    grad_queries = grad_queries.reshape(row_count, model_width).astype(jnp.bfloat16)
    grad_keys = (
        jnp.einsum("phqk,pqhd->pkhd", grad_scores, query_heads, preferred_element_type=jnp.float32)
        * score_scale
    )
    grad_keys = grad_keys.reshape(row_count, model_width).astype(jnp.bfloat16)
    grad_query_weight = matmul_tn(normed_one, grad_queries)
    grad_query_bias = column_sum(grad_queries)
    grad_key_weight = matmul_tn(normed_one, grad_keys)
    grad_value_weight = matmul_tn(normed_one, grad_values)
    grad_value_bias = column_sum(grad_values)
    grad_normed_one = (
        matmul_nt(grad_queries, query_weight)
        + matmul_nt(grad_keys, key_weight)
        + matmul_nt(grad_values, value_weight)
    )
    grad_from_one, grad_norm1_gain, grad_norm1_bias = norm_back(
        grad_normed_one, unit_one, inverse_one, norm1_gain.astype(jnp.float32)
    )
    grad_stream = grad_middle + grad_from_one
    grad_list = (
        grad_norm1_gain,
        grad_norm1_bias,
        grad_query_weight,
        grad_query_bias,
        grad_key_weight,
        grad_value_weight,
        grad_value_bias,
        grad_out_weight,
        grad_out_bias,
        grad_norm2_gain,
        grad_norm2_bias,
        grad_up_weight,
        grad_up_bias,
        grad_down_weight,
        grad_down_bias,
    )
    return (grad_stream, grad_list)


def body(
    block_input,
    embedding,
    out_grad,
    example_counts,
    example_lengths,
    norm1_gain,
    norm1_bias,
    query_weight,
    query_bias,
    key_weight,
    value_weight,
    value_bias,
    out_weight,
    out_bias,
    norm2_gain,
    norm2_bias,
    up_weight,
    up_bias,
    down_weight,
    down_bias,
):
    params = (
        norm1_gain,
        norm1_bias,
        query_weight,
        query_bias,
        key_weight,
        value_weight,
        value_bias,
        out_weight,
        out_bias,
        norm2_gain,
        norm2_bias,
        up_weight,
        up_bias,
        down_weight,
        down_bias,
    )
    row_slots = SLOTS * PER_ROW
    model_width = block_input.shape[1]
    micro_count = block_input.shape[0] // row_slots
    section_index = lax.axis_index("section")
    leading = section_index == 0
    example_iota = jnp.arange(MAXEX)
    used_slots = jnp.sum(
        jnp.where(example_iota[None, :] < example_counts[:, None], example_lengths, 0), axis=1
    )
    slot_iota = jnp.arange(SLOTS)
    causal = slot_iota[None, :] <= slot_iota[:, None]
    keep_all = causal[None] & (slot_iota[None, None, :] < used_slots[:, None, None])
    keep_all = keep_all.reshape(micro_count, PER_ROW, SLOTS, SLOTS)
    inputs = block_input.reshape(micro_count, row_slots, model_width)
    embeds = embedding.reshape(micro_count, row_slots, model_width)
    cotangents = out_grad.reshape(micro_count, row_slots, model_width)
    zero_sums = tuple((jnp.zeros(weight_arr.shape, jnp.float32) for weight_arr in params))

    def forward_turn(moment, carry):
        incoming, kept_streams, states = carry
        micro_index = moment - section_index
        slot_index = jnp.clip(micro_index, 0, micro_count - 1)
        active = (micro_index >= 0) & (micro_index < micro_count)
        carried = jnp.where(
            leading, inputs[slot_index].astype(jnp.float32), incoming.astype(jnp.float32)
        )
        stream = carried + embeds[slot_index].astype(jnp.float32)
        result, _ = forward_parts(stream, keep_all[slot_index], params)
        outgoing = result.astype(jnp.bfloat16)
        kept_streams = lax.dynamic_update_index_in_dim(
            kept_streams, jnp.where(active, stream, kept_streams[slot_index]), slot_index, 0
        )
        states = lax.dynamic_update_index_in_dim(
            states, jnp.where(active, outgoing, states[slot_index]), slot_index, 0
        )
        incoming = passed_along(outgoing, "section", 1)
        return (incoming, kept_streams, states)

    start_forward = (
        jnp.zeros((row_slots, model_width), jnp.bfloat16),
        jnp.zeros((micro_count, row_slots, model_width), jnp.float32),
        jnp.zeros((micro_count, row_slots, model_width), jnp.bfloat16),
    )
    _, kept_streams, states = lax.fori_loop(0, micro_count + 1, forward_turn, start_forward)

    def backward_turn(moment, carry):
        incoming, state_grads, grad_sums = carry
        micro_index = micro_count - 1 - moment + (1 - section_index)
        slot_index = jnp.clip(micro_index, 0, micro_count - 1)
        active = (micro_index >= 0) & (micro_index < micro_count)
        grad_result = jnp.where(
            leading, incoming.astype(jnp.float32), cotangents[slot_index].astype(jnp.float32)
        )
        grad_stream, grad_list = backward_parts(
            kept_streams[slot_index], keep_all[slot_index], grad_result, params
        )
        active_weight = active.astype(jnp.float32)
        grad_sums = tuple(
            (running + new_term * active_weight for running, new_term in zip(grad_sums, grad_list))
        )
        state_grads = lax.dynamic_update_index_in_dim(
            state_grads, jnp.where(active, grad_stream, state_grads[slot_index]), slot_index, 0
        )
        incoming = passed_along(grad_stream.astype(jnp.bfloat16), "section", -1)
        return (incoming, state_grads, grad_sums)

    start_backward = (
        jnp.zeros((row_slots, model_width), jnp.bfloat16),
        jnp.zeros((micro_count, row_slots, model_width), jnp.float32),
        zero_sums,
    )
    _, state_grads, grad_sums = lax.fori_loop(0, micro_count + 1, backward_turn, start_backward)
    totals = lax.psum(
        (
            grad_sums[0],
            grad_sums[1],
            grad_sums[2],
            grad_sums[3],
            grad_sums[4],
            grad_sums[5],
            grad_sums[6],
            grad_sums[7],
            grad_sums[8],
            grad_sums[9],
            grad_sums[10],
            grad_sums[11],
            grad_sums[12],
            grad_sums[13],
            grad_sums[14],
        ),
        ("section", "dp"),
    )
    states_out = states.reshape(1, micro_count * row_slots, model_width)
    grads_out = state_grads.reshape(1, micro_count * row_slots, model_width)
    return (
        states_out,
        grads_out,
        totals[0],
        totals[1],
        totals[2],
        totals[3],
        totals[4],
        totals[5],
        totals[6],
        totals[7],
        totals[8],
        totals[9],
        totals[10],
        totals[11],
        totals[12],
        totals[13],
        totals[14],
    )


def solution(mesh):
    placed = (
        P("dp", None),
        P("dp", None),
        P("dp", None),
        P("dp"),
        P("dp", None),
        P(),
        P(),
        P(),
        P(),
        P(),
        P(),
        P(),
        P(),
        P(),
        P(),
        P(),
        P(),
        P(),
        P(),
        P(),
    )
    return jax.shard_map(
        body,
        mesh=mesh,
        in_specs=placed,
        out_specs=(
            P("section", "dp", None),
            P("section", "dp", None),
            P(),
            P(),
            P(),
            P(),
            P(),
            P(),
            P(),
            P(),
            P(),
            P(),
            P(),
            P(),
            P(),
            P(),
            P(),
        ),
        check_vma=False,
    )
```

profile of v0, /device:TPU:0, one launch (start us, length us, event | category | flops | bytes accessed | tf_op | source)
XLA Modules:
  0.0 833.5 jit_solution(14588251343146118113)
XLA Ops:
  14.8 216.5 %while.65 = (s32[]{:T(128)}, bf16[1024,256]{0,1:T(8,128)(2,1)}, f32[4,1024,256]{1,2,0:T(8,128)}, bf16[4,1024,256]{2,1,0:T(8,128)(2,1)}, pred[]{:T(512)}, /*index...) while((s32[]{:T(128)}, bf16[1024,256]{0,1:T(8,128)(2,1)}, ...), condition=%wide.region_8.9_spmd, body=%wide.region_1.8_spmd.sunk | while | flops 1773147264 | bytes 64007144 | solution.py:325
  43.5 4.9 collective-permute-start
  50.8 8.7 %collective-permute-done = bf16[1024,256]{0,1:T(8,128)(2,1)S(1)} collective-permute-done((bf16[1024,256]{0,1:T(8,128)(2,1)S(1)}, bf16[1024,256]{0,1:T(8,128)(2,1)S(1)}, u32[]{:S(2)}, u32[]{:S(2)}) %collective-permute-start) | collective-permute-done | bytes 524320 | tf_op jit(solution)/shard_map/while/body/eval_jaxpr/ppermute | solution.py:15
  88.9 4.5 collective-permute-start
  95.8 7.9 collective-permute-done
  133.1 4.4 collective-permute-start
  139.9 6.9 collective-permute-done
  176.2 4.4 collective-permute-start
  183.1 6.0 collective-permute-done
  218.5 4.4 collective-permute-start
  225.4 5.1 collective-permute-done
  234.5 435.2 %while.66 = (s32[]{:T(128)}, bf16[1024,256]{0,1:T(8,128)(2,1)}, f32[4,1024,256]{2,1,0:T(8,128)}, f32[256]{0:T(256)}, f32[256]{0:T(256)}, /*index=5*/f32[256,256]...) while((s32[]{:T(128)}, bf16[1024,256]{0,1:T(8,128)(2,1)}, ...), condition=%wide.region_30.31_spmd.clone, body=%wide.region_9.30_spmd.clone.sunk | while | flops 4778101760 | bytes 245712800 | solution.py:353
  252.4 4.3 fusion.286
  262.6 4.1 convert_reduce_fusion.11
  273.0 4.9 convert_reduce_fusion.14
  293.0 3.3 multiply_reduce_fusion.24
  296.4 3.4 fusion.293
  302.6 3.4 fusion.299
  315.9 4.9 fusion.300
  338.8 4.3 fusion.286
  349.1 4.1 convert_reduce_fusion.11
  359.5 4.9 convert_reduce_fusion.14
  379.5 3.3 multiply_reduce_fusion.24
  382.9 3.4 fusion.293
  389.1 3.7 fusion.299
  402.8 5.2 fusion.300
  426.0 4.3 fusion.286
  436.3 4.1 convert_reduce_fusion.11
  446.7 4.9 convert_reduce_fusion.14
  466.7 3.3 multiply_reduce_fusion.24
  470.0 3.4 fusion.293
  476.2 3.7 fusion.299
  490.0 5.2 fusion.300
  513.2 4.3 fusion.286
  523.4 4.1 convert_reduce_fusion.11
  533.8 4.9 convert_reduce_fusion.14
  553.9 3.3 multiply_reduce_fusion.24
  557.2 3.4 fusion.293
  563.4 3.7 fusion.299
  577.2 5.2 fusion.300
  600.4 4.3 fusion.286
  610.6 4.1 convert_reduce_fusion.11
  621.0 4.9 convert_reduce_fusion.14
  644.4 3.4 fusion.293
  650.6 3.7 fusion.299
  664.3 5.2 fusion.300
  669.7 46.5 %all-reduce = (f32[256]{0:T(256)}, f32[256]{0:T(256)}, f32[256]{0:T(256)}, f32[256]{0:T(256)}, f32[256]{0:T(256)}, /*index=5*/f32[256]{0:T(256)}, f32[256]{0:T(256)}, f32[1024]{0:T(1024)}, f32[256]{0:T(256)}) all-reduce(f32[256]{0:T(256)} %get-tuple-element.2316, ...), channel_id=1, replica_groups=mesh['section'=2,'dp'=16] {'section','dp'}, use_global_device_ids=true, to_apply=%region_31.32 | all-reduce | flops 3072 | bytes 24576 | tf_op jit(solution)/shard_map/psum | solution.py:354
  716.2 100.4 %all-reduce.4.cloned.1.call-done = (f32[256,256]{1,0:T(8,128)}, f32[256,256]{1,0:T(8,128)}, f32[256,256]{1,0:T(8,128)}, f32[256,256]{1,0:T(8,128)}, f32[256,1024]{1,0:T(8,128)}, /*index=5*/f32[1024,256]{1,0:T(8,128)}) async-done(((f32[256,256]{1,0:T(8,128)}, f32[256,256]{1,0:T(8,128)}, f32[256,256]{1,0:T(8,128)}, f32[256,256]{1,0:T(8,128)}, f32[256,1024]{1,0:T(8,128)}, /*index=5*/f32[1024,256]{1,0:T(8,128)}), ...) | async-done | bytes 3145744 | tf_op jit(solution)/shard_map/psum | solution.py:354
  (1316 shorter events, 467.8 us)
Async XLA Ops:
  7.2 809.4 %all-reduce.4.cloned.1.call-start = ((), (), s32[]{:S(2)}) async-start(), calls=%async_computation | async-start | bytes 6291456 | tf_op jit(solution)/shard_map/psum | solution.py:354
  43.5 16.0 %collective-permute-start = (bf16[1024,256]{0,1:T(8,128)(2,1)S(1)}, bf16[1024,256]{0,1:T(8,128)(2,1)S(1)}, u32[]{:S(2)}, u32[]{:S(2)}) collective-permute-start(bf16[1024,256]{0,1:T(8,128)(2,1)S(1)} %fusion.245), channel_id=1, source_target_pairs={{0,16},{1,17},{2,18},{3,19},{4,20},{5,21},{6,22},{7,23},{8,24},{9,... | collective-permute-start | bytes 1572872 | tf_op jit(solution)/shard_map/while/body/eval_jaxpr/ppermute | solution.py:15
  88.9 14.8 %collective-permute-start = (bf16[1024,256]{0,1:T(8,128)(2,1)S(1)}, bf16[1024,256]{0,1:T(8,128)(2,1)S(1)}, u32[]{:S(2)}, u32[]{:S(2)}) collective-permute-start(bf16[1024,256]{0,1:T(8,128)(2,1)S(1)} %fusion.245), channel_id=1, source_target_pairs={{0,16},{1,17},{2,18},{3,19},{4,20},{5,21},{6,22},{7,23},{8,24},{9,... | collective-permute-start | bytes 1572872 | tf_op jit(solution)/shard_map/while/body/eval_jaxpr/ppermute | solution.py:15
  133.1 13.7 %collective-permute-start = (bf16[1024,256]{0,1:T(8,128)(2,1)S(1)}, bf16[1024,256]{0,1:T(8,128)(2,1)S(1)}, u32[]{:S(2)}, u32[]{:S(2)}) collective-permute-start(bf16[1024,256]{0,1:T(8,128)(2,1)S(1)} %fusion.245), channel_id=1, source_target_pairs={{0,16},{1,17},{2,18},{3,19},{4,20},{5,21},{6,22},{7,23},{8,24},{9,... | collective-permute-start | bytes 1572872 | tf_op jit(solution)/shard_map/while/body/eval_jaxpr/ppermute | solution.py:15
  176.2 12.9 %collective-permute-start = (bf16[1024,256]{0,1:T(8,128)(2,1)S(1)}, bf16[1024,256]{0,1:T(8,128)(2,1)S(1)}, u32[]{:S(2)}, u32[]{:S(2)}) collective-permute-start(bf16[1024,256]{0,1:T(8,128)(2,1)S(1)} %fusion.245), channel_id=1, source_target_pairs={{0,16},{1,17},{2,18},{3,19},{4,20},{5,21},{6,22},{7,23},{8,24},{9,... | collective-permute-start | bytes 1572872 | tf_op jit(solution)/shard_map/while/body/eval_jaxpr/ppermute | solution.py:15
  218.5 11.9 %collective-permute-start = (bf16[1024,256]{0,1:T(8,128)(2,1)S(1)}, bf16[1024,256]{0,1:T(8,128)(2,1)S(1)}, u32[]{:S(2)}, u32[]{:S(2)}) collective-permute-start(bf16[1024,256]{0,1:T(8,128)(2,1)S(1)} %fusion.245), channel_id=1, source_target_pairs={{0,16},{1,17},{2,18},{3,19},{4,20},{5,21},{6,22},{7,23},{8,24},{9,... | collective-permute-start | bytes 1572872 | tf_op jit(solution)/shard_map/while/body/eval_jaxpr/ppermute | solution.py:15
  236.4 13.5 %copy-start.34 = (f32[256]{0:T(256)}, f32[256]{0:T(256)S(1)}, u32[]{:S(2)}) copy-start(f32[256]{0:T(256)S(1)} %convert_element_type.854) | copy-start | bytes 3076 | tf_op jit(solution)/shard_map/while
  238.3 11.6 %copy-start.48 = (f32[256]{0:T(256)}, f32[256]{0:T(256)S(1)}, u32[]{:S(2)}) copy-start(f32[256]{0:T(256)S(1)} %convert_element_type.853) | copy-start | bytes 3076 | tf_op jit(solution)/shard_map/while
  249.5 13.1 %copy-start.18 = (bf16[1024,256]{0,1:T(8,128)(2,1)}, bf16[1024,256]{0,1:T(8,128)(2,1)S(1)}, u32[]{:S(2)}) copy-start(bf16[1024,256]{0,1:T(8,128)(2,1)S(1)} %get-tuple-element.2037) | copy-start | bytes 1572868 | tf_op jit(solution)/shard_map/while
  299.8 21.1 %collective-permute-start.1 = (bf16[1024,256]{0,1:T(8,128)(2,1)}, bf16[1024,256]{0,1:T(8,128)(2,1)}, u32[]{:S(2)}, u32[]{:S(2)}) collective-permute-start(bf16[1024,256]{0,1:T(8,128)(2,1)} %get-tuple-element.2050), channel_id=1, source_target_pairs={{16,0},{17,1},{18,2},{19,3},{20,4},{21,5},{22,6},{23,7},{24,8},{25... | collective-permute-start | bytes 1572872 | tf_op jit(solution)/shard_map/while/body/eval_jaxpr/ppermute | solution.py:15
  322.9 13.5 %copy-start.34 = (f32[256]{0:T(256)}, f32[256]{0:T(256)S(1)}, u32[]{:S(2)}) copy-start(f32[256]{0:T(256)S(1)} %convert_element_type.854) | copy-start | bytes 3076 | tf_op jit(solution)/shard_map/while
  324.8 11.6 %copy-start.48 = (f32[256]{0:T(256)}, f32[256]{0:T(256)S(1)}, u32[]{:S(2)}) copy-start(f32[256]{0:T(256)S(1)} %convert_element_type.853) | copy-start | bytes 3076 | tf_op jit(solution)/shard_map/while
  336.0 13.1 %copy-start.18 = (bf16[1024,256]{0,1:T(8,128)(2,1)}, bf16[1024,256]{0,1:T(8,128)(2,1)S(1)}, u32[]{:S(2)}) copy-start(bf16[1024,256]{0,1:T(8,128)(2,1)S(1)} %get-tuple-element.2037) | copy-start | bytes 1572868 | tf_op jit(solution)/shard_map/while
  386.3 21.8 %collective-permute-start.1 = (bf16[1024,256]{0,1:T(8,128)(2,1)}, bf16[1024,256]{0,1:T(8,128)(2,1)}, u32[]{:S(2)}, u32[]{:S(2)}) collective-permute-start(bf16[1024,256]{0,1:T(8,128)(2,1)} %get-tuple-element.2050), channel_id=1, source_target_pairs={{16,0},{17,1},{18,2},{19,3},{20,4},{21,5},{22,6},{23,7},{24,8},{25... | collective-permute-start | bytes 1572872 | tf_op jit(solution)/shard_map/while/body/eval_jaxpr/ppermute | solution.py:15
  394.2 8.5 %copy-start.51 = (f32[256]{0:T(256)S(1)}, f32[256]{0:T(256)}, u32[]{:S(2)}) copy-start(f32[256]{0:T(256)} %get-tuple-element.2052) | copy-start | bytes 3076 | tf_op jit(solution)/shard_map/while
  394.2 8.5 %copy-start.67 = (f32[256]{0:T(256)S(1)}, f32[256]{0:T(256)}, u32[]{:S(2)}) copy-start(f32[256]{0:T(256)} %get-tuple-element.2192) | copy-start | bytes 3076 | tf_op jit(solution)/shard_map/while
  394.2 8.5 %copy-start.50 = (f32[256]{0:T(256)S(1)}, f32[256]{0:T(256)}, u32[]{:S(2)}) copy-start(f32[256]{0:T(256)} %get-tuple-element.2053) | copy-start | bytes 3076 | tf_op jit(solution)/shard_map/while
  394.2 8.5 %copy-start.65 = (f32[256]{0:T(256)S(1)}, f32[256]{0:T(256)}, u32[]{:S(2)}) copy-start(f32[256]{0:T(256)} %get-tuple-element.2193) | copy-start | bytes 3076 | tf_op jit(solution)/shard_map/while
  394.2 8.5 %copy-start.19 = (bf16[1024,256]{0,1:T(8,128)(2,1)S(1)}, bf16[1024,256]{0,1:T(8,128)(2,1)}, u32[]{:S(2)}) copy-start(bf16[1024,256]{0,1:T(8,128)(2,1)} %copy-done.18) | copy-start | bytes 1572868 | tf_op jit(solution)/shard_map/while
  394.2 8.5 %copy-start.45 = (f32[1024]{0:T(1024)S(1)}, f32[1024]{0:T(1024)}, u32[]{:S(2)}) copy-start(f32[1024]{0:T(1024)} %convert_element_type.859) | copy-start | bytes 12292 | tf_op jit(solution)/shard_map/while
  410.0 13.5 %copy-start.34 = (f32[256]{0:T(256)}, f32[256]{0:T(256)S(1)}, u32[]{:S(2)}) copy-start(f32[256]{0:T(256)S(1)} %convert_element_type.854) | copy-start | bytes 3076 | tf_op jit(solution)/shard_map/while
  412.0 11.6 %copy-start.48 = (f32[256]{0:T(256)}, f32[256]{0:T(256)S(1)}, u32[]{:S(2)}) copy-start(f32[256]{0:T(256)S(1)} %convert_element_type.853) | copy-start | bytes 3076 | tf_op jit(solution)/shard_map/while
  423.1 13.1 %copy-start.18 = (bf16[1024,256]{0,1:T(8,128)(2,1)}, bf16[1024,256]{0,1:T(8,128)(2,1)S(1)}, u32[]{:S(2)}) copy-start(bf16[1024,256]{0,1:T(8,128)(2,1)S(1)} %get-tuple-element.2037) | copy-start | bytes 1572868 | tf_op jit(solution)/shard_map/while
  473.4 21.8 %collective-permute-start.1 = (bf16[1024,256]{0,1:T(8,128)(2,1)}, bf16[1024,256]{0,1:T(8,128)(2,1)}, u32[]{:S(2)}, u32[]{:S(2)}) collective-permute-start(bf16[1024,256]{0,1:T(8,128)(2,1)} %get-tuple-element.2050), channel_id=1, source_target_pairs={{16,0},{17,1},{18,2},{19,3},{20,4},{21,5},{22,6},{23,7},{24,8},{25... | collective-permute-start | bytes 1572872 | tf_op jit(solution)/shard_map/while/body/eval_jaxpr/ppermute | solution.py:15
  481.4 8.5 %copy-start.51 = (f32[256]{0:T(256)S(1)}, f32[256]{0:T(256)}, u32[]{:S(2)}) copy-start(f32[256]{0:T(256)} %get-tuple-element.2052) | copy-start | bytes 3076 | tf_op jit(solution)/shard_map/while
  481.4 8.5 %copy-start.67 = (f32[256]{0:T(256)S(1)}, f32[256]{0:T(256)}, u32[]{:S(2)}) copy-start(f32[256]{0:T(256)} %get-tuple-element.2192) | copy-start | bytes 3076 | tf_op jit(solution)/shard_map/while
  481.4 8.5 %copy-start.50 = (f32[256]{0:T(256)S(1)}, f32[256]{0:T(256)}, u32[]{:S(2)}) copy-start(f32[256]{0:T(256)} %get-tuple-element.2053) | copy-start | bytes 3076 | tf_op jit(solution)/shard_map/while
  481.4 8.5 %copy-start.65 = (f32[256]{0:T(256)S(1)}, f32[256]{0:T(256)}, u32[]{:S(2)}) copy-start(f32[256]{0:T(256)} %get-tuple-element.2193) | copy-start | bytes 3076 | tf_op jit(solution)/shard_map/while
  481.4 8.5 %copy-start.19 = (bf16[1024,256]{0,1:T(8,128)(2,1)S(1)}, bf16[1024,256]{0,1:T(8,128)(2,1)}, u32[]{:S(2)}) copy-start(bf16[1024,256]{0,1:T(8,128)(2,1)} %copy-done.18) | copy-start | bytes 1572868 | tf_op jit(solution)/shard_map/while
  481.4 8.5 %copy-start.45 = (f32[1024]{0:T(1024)S(1)}, f32[1024]{0:T(1024)}, u32[]{:S(2)}) copy-start(f32[1024]{0:T(1024)} %convert_element_type.859) | copy-start | bytes 12292 | tf_op jit(solution)/shard_map/while
  497.2 13.5 %copy-start.34 = (f32[256]{0:T(256)}, f32[256]{0:T(256)S(1)}, u32[]{:S(2)}) copy-start(f32[256]{0:T(256)S(1)} %convert_element_type.854) | copy-start | bytes 3076 | tf_op jit(solution)/shard_map/while
  499.1 11.6 %copy-start.48 = (f32[256]{0:T(256)}, f32[256]{0:T(256)S(1)}, u32[]{:S(2)}) copy-start(f32[256]{0:T(256)S(1)} %convert_element_type.853) | copy-start | bytes 3076 | tf_op jit(solution)/shard_map/while
  510.3 13.1 %copy-start.18 = (bf16[1024,256]{0,1:T(8,128)(2,1)}, bf16[1024,256]{0,1:T(8,128)(2,1)S(1)}, u32[]{:S(2)}) copy-start(bf16[1024,256]{0,1:T(8,128)(2,1)S(1)} %get-tuple-element.2037) | copy-start | bytes 1572868 | tf_op jit(solution)/shard_map/while
  560.6 21.8 %collective-permute-start.1 = (bf16[1024,256]{0,1:T(8,128)(2,1)}, bf16[1024,256]{0,1:T(8,128)(2,1)}, u32[]{:S(2)}, u32[]{:S(2)}) collective-permute-start(bf16[1024,256]{0,1:T(8,128)(2,1)} %get-tuple-element.2050), channel_id=1, source_target_pairs={{16,0},{17,1},{18,2},{19,3},{20,4},{21,5},{22,6},{23,7},{24,8},{25... | collective-permute-start | bytes 1572872 | tf_op jit(solution)/shard_map/while/body/eval_jaxpr/ppermute | solution.py:15
  568.5 8.5 %copy-start.51 = (f32[256]{0:T(256)S(1)}, f32[256]{0:T(256)}, u32[]{:S(2)}) copy-start(f32[256]{0:T(256)} %get-tuple-element.2052) | copy-start | bytes 3076 | tf_op jit(solution)/shard_map/while
  568.6 8.5 %copy-start.50 = (f32[256]{0:T(256)S(1)}, f32[256]{0:T(256)}, u32[]{:S(2)}) copy-start(f32[256]{0:T(256)} %get-tuple-element.2053) | copy-start | bytes 3076 | tf_op jit(solution)/shard_map/while
  568.6 8.5 %copy-start.65 = (f32[256]{0:T(256)S(1)}, f32[256]{0:T(256)}, u32[]{:S(2)}) copy-start(f32[256]{0:T(256)} %get-tuple-element.2193) | copy-start | bytes 3076 | tf_op jit(solution)/shard_map/while
  568.6 8.5 %copy-start.19 = (bf16[1024,256]{0,1:T(8,128)(2,1)S(1)}, bf16[1024,256]{0,1:T(8,128)(2,1)}, u32[]{:S(2)}) copy-start(bf16[1024,256]{0,1:T(8,128)(2,1)} %copy-done.18) | copy-start | bytes 1572868 | tf_op jit(solution)/shard_map/while
  568.6 8.5 %copy-start.45 = (f32[1024]{0:T(1024)S(1)}, f32[1024]{0:T(1024)}, u32[]{:S(2)}) copy-start(f32[1024]{0:T(1024)} %convert_element_type.859) | copy-start | bytes 12292 | tf_op jit(solution)/shard_map/while
  584.4 13.5 %copy-start.34 = (f32[256]{0:T(256)}, f32[256]{0:T(256)S(1)}, u32[]{:S(2)}) copy-start(f32[256]{0:T(256)S(1)} %convert_element_type.854) | copy-start | bytes 3076 | tf_op jit(solution)/shard_map/while
  586.3 11.6 %copy-start.48 = (f32[256]{0:T(256)}, f32[256]{0:T(256)S(1)}, u32[]{:S(2)}) copy-start(f32[256]{0:T(256)S(1)} %convert_element_type.853) | copy-start | bytes 3076 | tf_op jit(solution)/shard_map/while
  597.5 13.1 %copy-start.18 = (bf16[1024,256]{0,1:T(8,128)(2,1)}, bf16[1024,256]{0,1:T(8,128)(2,1)S(1)}, u32[]{:S(2)}) copy-start(bf16[1024,256]{0,1:T(8,128)(2,1)S(1)} %get-tuple-element.2037) | copy-start | bytes 1572868 | tf_op jit(solution)/shard_map/while
  647.8 21.8 %collective-permute-start.1 = (bf16[1024,256]{0,1:T(8,128)(2,1)}, bf16[1024,256]{0,1:T(8,128)(2,1)}, u32[]{:S(2)}, u32[]{:S(2)}) collective-permute-start(bf16[1024,256]{0,1:T(8,128)(2,1)} %get-tuple-element.2050), channel_id=1, source_target_pairs={{16,0},{17,1},{18,2},{19,3},{20,4},{21,5},{22,6},{23,7},{24,8},{25... | collective-permute-start | bytes 1572872 | tf_op jit(solution)/shard_map/while/body/eval_jaxpr/ppermute | solution.py:15
  655.8 8.5 %copy-start.50 = (f32[256]{0:T(256)S(1)}, f32[256]{0:T(256)}, u32[]{:S(2)}) copy-start(f32[256]{0:T(256)} %get-tuple-element.2053) | copy-start | bytes 3076 | tf_op jit(solution)/shard_map/while
  655.8 8.5 %copy-start.65 = (f32[256]{0:T(256)S(1)}, f32[256]{0:T(256)}, u32[]{:S(2)}) copy-start(f32[256]{0:T(256)} %get-tuple-element.2193) | copy-start | bytes 3076 | tf_op jit(solution)/shard_map/while
  655.8 8.5 %copy-start.19 = (bf16[1024,256]{0,1:T(8,128)(2,1)S(1)}, bf16[1024,256]{0,1:T(8,128)(2,1)}, u32[]{:S(2)}) copy-start(bf16[1024,256]{0,1:T(8,128)(2,1)} %copy-done.18) | copy-start | bytes 1572868 | tf_op jit(solution)/shard_map/while
  655.8 8.5 %copy-start.45 = (f32[1024]{0:T(1024)S(1)}, f32[1024]{0:T(1024)}, u32[]{:S(2)}) copy-start(f32[1024]{0:T(1024)} %convert_element_type.859) | copy-start | bytes 12292 | tf_op jit(solution)/shard_map/while
  816.6 9.1 %copy-start.30 = (f32[1024,256]{1,0:T(8,128)S(1)}, f32[1024,256]{1,0:T(8,128)}, u32[]{:S(2)}) copy-start(f32[1024,256]{1,0:T(8,128)} %get-tuple-element.2286) | copy-start | bytes 3145732
  (304 other events, 1466.0 us)
Sparse Core Ops, SparseCore 0:
  669.8 146.7 all-reduce.3
where the time goes:
time: 841 us; the launch traced here: 833 us
  matrix products  237 us (28%)
  other arithmetic  210 us (25%)
  local copies, waits for them, and re-layouts  155 us (18%)
  waiting for transfers between devices  135 us (16%)
  blocking collectives  46.5 us (6%)
  starting transfers between devices  29.1 us (3%)
  between operations  14.2 us (2%)
    psum x1, waiting for transfers between devices, body(): lax.psum((grad_sums[0], grad_sums[1], grad_sums[2], grad_sums[3], grad_su...  100 us
    dot_general x30, matrix products, matmul_tn(): lax.dot_general(left_op, right_op, (((0,), (0,)), ((), ())), preferred_el...  70 us
    dot_general x30, matrix products, matmul_nt(): lax.dot_general(left_op, right_op, (((1,), (1,)), ((), ())), preferred_el...  54 us
    dot_general x50, matrix products, matmul(): return jnp.dot(left_op, right_op, preferred_element_type=jnp.float32)  49.3 us
    psum x1, blocking collectives, body(): lax.psum((grad_sums[0], grad_sums[1], grad_sums[2], grad_sums[3], grad_su...  46.5 us
    ppermute x10, waiting for transfers between devices, passed_along(): return lax.ppermute(block, axis, route)  34.7 us
    ppermute x10, starting transfers between devices, passed_along(): return lax.ppermute(block, axis, route)  29 us
    sub x10, other arithmetic, forward_parts(): shifted = jnp.exp(scores - row_max)  28.1 us
  transfers between devices with their start and end apart: 11, of which 6 were waited for; matrix products, arithmetic and copies ran while one was open for 12% of the time, Pallas kernels for 0%

commit v1 on v0

v1 whole, which is shorter than its diff:
```python
import functools
import math

import jax
import jax.numpy as jnp
from jax import lax
from jax.experimental import pallas as pl
from jax.experimental.pallas import tpu as pltpu
from jax.sharding import PartitionSpec as P

BF = jnp.bfloat16
F32 = jnp.float32
SLOTS = 128
HEADS = 8
KEYS = 112
GROUP = 256
EPS = 1e-5


def nn(a, b):
    return lax.dot_general(a, b, (((1,), (0,)), ((), ())), preferred_element_type=F32)


def nt(a, b):
    return lax.dot_general(a, b, (((1,), (1,)), ((), ())), preferred_element_type=F32)


def ln_forward(u, gain, bias, unit_ref, inv_ref, n_ref):
    d = u.shape[0]
    mean = jnp.sum(u, axis=0, keepdims=True) * (1.0 / d)
    c = u - mean
    var = jnp.sum(c * c, axis=0, keepdims=True) * (1.0 / d)
    inv = lax.rsqrt(var + EPS)
    unit = c * inv
    unit_ref[...] = unit
    inv_ref[...] = inv
    n_ref[0:d, :] = (unit * gain + bias).astype(BF)


def lanes2(ref):
    v = ref[...]
    return jnp.concatenate([v, v], axis=1)


def fold(v):
    return v[:, :128] + v[:, 128:]


def ln_backward(gn, unit, inv, gain, gain_acc, bias_acc):
    d = gn.shape[0]
    t = gn * unit
    gain_acc[...] += fold(t)
    bias_acc[...] += fold(gn)
    s = gn * gain
    m1 = jnp.sum(s, axis=0, keepdims=True) * (1.0 / d)
    m2 = jnp.sum(t * gain, axis=0, keepdims=True) * (1.0 / d)
    return inv * (s - m1 - unit * m2)


C0 = math.sqrt(2.0 / math.pi)
C1 = C0 * 0.044715


def kernel(off_ref, x_ref, e_ref, g_ref, used_ref,
           n1g_ref, n1b_ref, wq_ref, qb_ref, wk_ref, wv_ref, vb_ref, wo_ref, ob_ref,
           n2g_ref, n2b_ref, wu_ref, ub_ref, wd_ref, db_ref,
           st_ref, gr_ref, awd_ref, awu_ref, awqkv_ref, awo_ref, aln_ref,
           wqkvT, woT, wuT, wdT, wqkv, vecs, ubv,
           n1T, qkvT, vN, p32, p16, mixT, unit1, inv1, unit2, inv2, n2T, gp, hT,
           bd, ds16, dqkvT, goT, aln):
    step = pl.program_id(0)
    steps = pl.num_programs(0)
    D = 256
    FF = 1024
    scale = 32 ** -0.5

    @pl.when(step == 0)
    def _():
        wqkvT[0:256, :] = wq_ref[...].T
        wqkvT[256:512, :] = wk_ref[...].T
        wqkvT[512:768, :] = wv_ref[...].T
        woT[...] = wo_ref[...].T
        wuT[...] = wu_ref[...].T
        wdT[...] = wd_ref[...].T
        wqkv[:, 0:256] = wq_ref[...]
        wqkv[:, 256:512] = wk_ref[...]
        wqkv[:, 512:768] = wv_ref[...]
        for i, r in enumerate((n1g_ref, n1b_ref, qb_ref, vb_ref, ob_ref, n2g_ref, n2b_ref, db_ref)):
            vecs[i] = jnp.broadcast_to(r[...].astype(F32), (128, D)).T
        ubv[...] = jnp.broadcast_to(ub_ref[...].astype(F32), (128, FF)).T
        awd_ref[...] = jnp.zeros_like(awd_ref)
        awu_ref[...] = jnp.zeros_like(awu_ref)
        awqkv_ref[...] = jnp.zeros_like(awqkv_ref)
        awo_ref[...] = jnp.zeros_like(awo_ref)
        aln[...] = jnp.zeros_like(aln)
        bd[...] = jnp.zeros_like(bd)
        ds16[...] = jnp.zeros_like(ds16)
        p16[...] = jnp.zeros_like(p16)
        for it in range(2):
            n1T[it, D:, :] = jnp.ones((16, GROUP), BF)
            mixT[it, D:, :] = jnp.ones((16, GROUP), BF)
            n2T[it, D:, :] = jnp.ones((16, GROUP), BF)
            hT[it, FF:, :] = jnp.ones((16, GROUP), BF)

    k_iota = lax.broadcasted_iota(jnp.int32, (KEYS, SLOTS), 0)
    q_iota = lax.broadcasted_iota(jnp.int32, (KEYS, SLOTS), 1)
    masks = []
    for p in range(2):
        used = used_ref[step * 2 + p]
        masks.append(jnp.where((k_iota <= q_iota) & (k_iota < used), 0.0, -1e30).astype(F32))

    def forward(u, it):
        ln_forward(u, lanes2(vecs.at[0]), lanes2(vecs.at[1]), unit1.at[it], inv1.at[it], n1T.at[it])
        n1 = n1T[it, 0:D, :]
        qkvT[it, 0:256, :] = (nn(wqkvT[0:256, :], n1) + lanes2(vecs.at[2])).astype(BF)
        qkvT[it, 256:512, :] = nn(wqkvT[256:512, :], n1).astype(BF)
        qkvT[it, 512:768, :] = (nn(wqkvT[512:768, :], n1) + lanes2(vecs.at[3])).astype(BF)
        for p in range(2):
            tok = slice(p * 128, p * 128 + 128)
            kN = qkvT[it, 256:512, tok].T
            vN[it, p] = qkvT[it, 512:768, tok].T
            for h in range(HEADS):
                bd[p, 32 * h:32 * h + 32, 128 * h:128 * h + 128] = qkvT[it, 32 * h:32 * h + 32, tok]
            for h2 in range(HEADS // 2):
                sT2 = nn(kN[:KEYS], bd[p, :, 256 * h2:256 * h2 + 256])
                for hh in range(2):
                    h = h2 * 2 + hh
                    ln = slice(128 * h, 128 * h + 128)
                    s = sT2[:, 128 * hh:128 * hh + 128] + masks[p]
                    m = jnp.max(s, axis=0, keepdims=True)
                    pe = jnp.exp2((s - m) * (scale * math.log2(math.e)))
                    l = jnp.sum(pe, axis=0, keepdims=True)
                    pT = pe * (1.0 / l)
                    p32[it, p, :, ln] = pT
                    p16[it, p, 0:KEYS, ln] = pT.astype(BF)
                    o = nn(qkvT[it, 512 + 32 * h:544 + 32 * h, tok], p16[it, p, :, ln])
                    mixT[it, 32 * h:32 * h + 32, tok] = o.astype(BF)
        middle = u + nn(woT[...], mixT[it, 0:D, :]) + lanes2(vecs.at[4])
        ln_forward(middle, lanes2(vecs.at[5]), lanes2(vecs.at[6]), unit2.at[it], inv2.at[it], n2T.at[it])
        n2 = n2T[it, 0:D, :]
        for c in range(FF // 128):
            rows = slice(c * 128, c * 128 + 128)
            v = nn(wuT[rows, :], n2) + lanes2(ubv.at[rows])
            v2 = v * v
            t = jnp.tanh(v * (C0 + C1 * v2))
            h1 = 0.5 + 0.5 * t
            hid = v * h1
            gp[it, rows, :] = h1 + (hid - hid * h1) * (2.0 * C0 + 6.0 * C1 * v2)
            hT[it, rows, :] = hid.astype(BF)
        return middle + nn(wdT[...], hT[it, 0:FF, :]) + lanes2(vecs.at[7])

    def backward(g, it):
        low = g.astype(BF)
        awd_ref[...] += nt(hT[it], low)
        for c in range(FF // 128):
            rows = slice(c * 128, c * 128 + 128)
            dh = nn(wd_ref[rows, :], low)
            goT[rows, :] = (dh * gp[it, rows, :]).astype(BF)
        dpre = goT[...]
        awu_ref[...] += nt(n2T[it], dpre)
        dn2 = nn(wu_ref[...], dpre)
        dmid = g + ln_backward(dn2, unit2[it], inv2[it], lanes2(vecs.at[5]), aln.at[2], aln.at[3])
        alow = dmid.astype(BF)
        awo_ref[...] += nt(mixT[it], alow)
        dmix = nn(wo_ref[...], alow).astype(BF)
        for p in range(2):
            tok = slice(p * 128, p * 128 + 128)
            for h in range(HEADS):
                bd[p, 32 * h:32 * h + 32, 128 * h:128 * h + 128] = dmix[32 * h:32 * h + 32, tok]
            for h2 in range(HEADS // 2):
                dp2 = nn(vN[it, p, 0:KEYS, :], bd[p, :, 256 * h2:256 * h2 + 256])
                for hh in range(2):
                    h = h2 * 2 + hh
                    ln = slice(128 * h, 128 * h + 128)
                    hr = slice(32 * h, 32 * h + 32)
                    pT = p32[it, p, :, ln]
                    t = pT * dp2[:, 128 * hh:128 * hh + 128]
                    dsum = jnp.sum(t, axis=0, keepdims=True)
                    ds16[p, 0:KEYS, ln] = (t - pT * dsum).astype(BF)
                    ds = ds16[p, :, ln]
                    dqkvT[32 * h:32 * h + 32, tok] = (nn(qkvT[it, 256 + 32 * h:288 + 32 * h, tok], ds) * scale).astype(BF)
                    dqkvT[256 + 32 * h:288 + 32 * h, tok] = (nt(qkvT[it, hr, tok], ds) * scale).astype(BF)
                    dqkvT[512 + 32 * h:544 + 32 * h, tok] = nt(dmix[hr, tok], p16[it, p, :, ln]).astype(BF)
        dqkv = dqkvT[...]
        awqkv_ref[...] += nt(n1T[it], dqkv)
        dn1 = nn(wqkv[...], dqkv)
        return dmid + ln_backward(dn1, unit1[it], inv1[it], lanes2(vecs.at[0]), aln.at[0], aln.at[1])

    eT = e_ref[...].T.astype(F32)
    u1 = x_ref[...].T.astype(F32) + eT
    s1 = forward(u1, 0).astype(BF)
    st_ref[0] = s1.T
    u2 = s1.astype(F32) + eT
    s2 = forward(u2, 1).astype(BF)
    st_ref[1] = s2.T
    g2 = backward(g_ref[...].T.astype(F32), 1)
    g2l = g2.astype(BF)
    gr_ref[1] = g2l.T
    g1 = backward(g2l.astype(F32), 0)
    gr_ref[0] = g1.astype(BF).T

    @pl.when(step == steps - 1)
    def _():
        for i in range(4):
            aln_ref[i:i + 1, :] = jnp.sum(aln[i].T, axis=0, keepdims=True)


def compute(offset, x, e, g, used, params, rows):
    (n1g, n1b, wq, qb, wk, wv, vb, wo, ob, n2g, n2b, wu, ub, wd, db) = params
    row = lambda v: v.reshape(1, -1)
    steps = rows // GROUP
    blk = pl.BlockSpec((GROUP, 256), lambda i, off: (off[0] + i, 0))
    full = lambda a: pl.BlockSpec(a.shape, lambda i, off: (0,) * a.ndim)
    ws = [row(n1g), row(n1b), wq, row(qb), wk, wv, row(vb), wo, row(ob), row(n2g), row(n2b), wu, row(ub), wd, row(db)]
    outs = [
        jax.ShapeDtypeStruct((2, rows, 256), BF),
        jax.ShapeDtypeStruct((2, rows, 256), BF),
        jax.ShapeDtypeStruct((1040, 256), F32),
        jax.ShapeDtypeStruct((272, 1024), F32),
        jax.ShapeDtypeStruct((272, 768), F32),
        jax.ShapeDtypeStruct((272, 256), F32),
        jax.ShapeDtypeStruct((8, 256), F32),
    ]
    oblk = pl.BlockSpec((2, GROUP, 256), lambda i, off: (0, i, 0))
    return pl.pallas_call(
        kernel,
        out_shape=outs,
        grid_spec=pltpu.PrefetchScalarGridSpec(
            num_scalar_prefetch=1,
            grid=(steps,),
            in_specs=[blk, blk, blk, pl.BlockSpec(memory_space=pltpu.SMEM)] + [full(w) for w in ws],
            out_specs=[oblk, oblk] + [full(o) for o in outs[2:]],
            scratch_shapes=[
                pltpu.VMEM((768, 256), BF), pltpu.VMEM((256, 256), BF), pltpu.VMEM((1024, 256), BF),
                pltpu.VMEM((256, 1024), BF), pltpu.VMEM((256, 768), BF),
                pltpu.VMEM((8, 256, 128), F32), pltpu.VMEM((1024, 128), F32),
                pltpu.VMEM((2, 272, GROUP), BF),
                pltpu.VMEM((2, 768, GROUP), BF),
                pltpu.VMEM((2, 2, 128, 256), BF),
                pltpu.VMEM((2, 2, KEYS, 1024), F32),
                pltpu.VMEM((2, 2, 128, 1024), BF),
                pltpu.VMEM((2, 272, GROUP), BF),
                pltpu.VMEM((2, 256, GROUP), F32), pltpu.VMEM((2, 1, GROUP), F32),
                pltpu.VMEM((2, 256, GROUP), F32), pltpu.VMEM((2, 1, GROUP), F32),
                pltpu.VMEM((2, 272, GROUP), BF),
                pltpu.VMEM((2, 1024, GROUP), F32),
                pltpu.VMEM((2, 1040, GROUP), BF),
                pltpu.VMEM((2, 256, 1024), BF),
                pltpu.VMEM((2, 128, 1024), BF),
                pltpu.VMEM((768, GROUP), BF),
                pltpu.VMEM((1024, GROUP), BF),
                pltpu.VMEM((4, 256, 128), F32),
            ],
        ),
        compiler_params=pltpu.CompilerParams(vmem_limit_bytes=56 * 1024 * 1024),
    )(offset, x, e, g, used, *ws)


def body(block_input, embedding, out_grad, example_counts, example_lengths, *params):
    section = lax.axis_index("section")
    local = block_input.shape[0]
    rows = local // 2
    prompts = rows // SLOTS
    counts = lax.dynamic_slice_in_dim(example_counts, section * prompts, prompts, 0)
    lengths = lax.dynamic_slice_in_dim(example_lengths, section * prompts, prompts, 0)
    slots = jnp.arange(lengths.shape[1])
    used = jnp.sum(jnp.where(slots[None, :] < counts[:, None], lengths, 0), axis=1)
    offset = (section * (rows // GROUP)).astype(jnp.int32).reshape(1)
    st, gr, awd, awu, awqkv, awo, aln = compute(offset, block_input, embedding, out_grad, used, params, rows)

    def exchange(pair):
        mine = lax.dynamic_index_in_dim(pair, section, 0, keepdims=False)
        other = lax.dynamic_index_in_dim(pair, 1 - section, 0, keepdims=False)
        got = lax.ppermute(other, "section", [(0, 1), (1, 0)])
        first = jnp.where(section == 0, mine, got)
        second = jnp.where(section == 0, got, mine)
        return jnp.concatenate([first, second], axis=0)[None]

    awd, awu, awqkv, awo, aln = lax.psum((awd, awu, awqkv, awo, aln), ("section", "dp"))
    return (
        exchange(st),
        exchange(gr).astype(F32),
        aln[0],
        aln[1],
        awqkv[:256, :256],
        awqkv[256, :256],
        awqkv[:256, 256:512],
        awqkv[:256, 512:],
        awqkv[256, 512:],
        awo[:256],
        awo[256],
        aln[2],
        aln[3],
        awu[:256],
        awu[256],
        awd[:1024],
        awd[1024],
    )


def solution(mesh):
    placed = (P("dp", None),) * 3 + (P("dp"), P("dp", None)) + (P(),) * 15
    return jax.shard_map(
        body,
        mesh=mesh,
        in_specs=placed,
        out_specs=(P("section", "dp", None),) * 2 + (P(),) * 15,
        check_vma=False,
    )
```

time: 841 us -> 291 us (0.35)
  matrix products: 237 us -> 0 us
  other arithmetic: 210 us -> 7.01 us
  local copies, waits for them, and re-layouts: 155 us -> 26.2 us
  Pallas kernels: 0 us -> 102 us
  waiting for transfers between devices: 135 us -> 49.5 us
  blocking collectives: 46.5 us -> 88.2 us
  starting transfers between devices: 29.1 us -> 3.01 us
    dot_general x150 -> x0, matrix products: 237 us -> none  [the longest x30 70 us: matmul_tn(): lax.dot_general(left_op, right_op, (((0,), (0,)), ((), ())), preferred_el...]
    pallas_call x0 -> x1, Pallas kernels: none -> 102 us  [compute(): pl.pallas_call(kernel, out_shape=outs, grid_spec=pltpu.PrefetchScalarGrid...]
    convert_element_type x100 -> x1, other arithmetic: 102 us -> 2.34 us  [body(): exchange(gr).astype(F32)]
    psum x1, waiting for transfers between devices: 100 us -> 49.4 us  [body(): lax.psum((awd, awu, awqkv, awo, aln), ('section', 'dp'))]
    reduce_sum x46 -> x1, other arithmetic: 48.4 us -> 1.39 us  [body(): jnp.sum(jnp.where(slots[None, :] < counts[:, None], lengths, 0), axis=1)]
    psum x1, blocking collectives: 46.5 us -> 88.2 us  [body(): lax.psum((awd, awu, awqkv, awo, aln), ('section', 'dp'))]
    dynamic_slice x50 -> x1, local copies, waits for them, and re-layouts: 40.7 us -> 0.73 us  [body(): lax.dynamic_slice_in_dim(example_counts, section * prompts, prompts, 0)]
    ppermute x10 -> x2, waiting for transfers between devices: 34.7 us -> 0.01 us  [exchange(): got = lax.ppermute(other, 'section', [(0, 1), (1, 0)])]
  transfers between devices with their start and end apart: 11 -> 3, of which waited for: 6 -> 1; matrix products, arithmetic and copies ran while one was open for 12% -> 2% of each run, Pallas kernels for 0% -> 0%
where the time goes in v1:
time: 291 us; the launch traced here: 290 us
  Pallas kernels  102 us (35%)
  blocking collectives  88.2 us (30%)
  waiting for transfers between devices  49.5 us (17%)
  local copies, waits for them, and re-layouts  26.2 us (9%)
  between operations  14.1 us (5%)
  other arithmetic  7.01 us (2%)
  starting transfers between devices  3.01 us (1%)
    pallas_call x1, Pallas kernels, compute(): pl.pallas_call(kernel, out_shape=outs, grid_spec=pltpu.PrefetchScalarGrid...  102 us
    psum x1, blocking collectives, body(): lax.psum((awd, awu, awqkv, awo, aln), ('section', 'dp'))  88.2 us
    psum x1, waiting for transfers between devices, body(): lax.psum((awd, awu, awqkv, awo, aln), ('section', 'dp'))  49.4 us
    reshape x9, local copies, waits for them, and re-layouts, compute(): row = lambda v: v.reshape(1, -1)  11 us
  transfers between devices with their start and end apart: 3, of which 1 were waited for; matrix products, arithmetic and copies ran while one was open for 2% of the time, Pallas kernels for 0%

profile of v1, /device:TPU:0, one launch (start us, length us, event | category | flops | bytes accessed | tf_op | source)
XLA Modules:
  0.0 290.4 jit_solution(10714582645172527300)
XLA Ops:
  7.2 0.0 all-reduce.3.cloned.1.call-start
  7.2 1.2 reshape.96.n1g_ref
  8.5 1.2 reshape.97.n1b_ref
  9.7 1.2 reshape.98.qb_ref
  10.9 1.2 reshape.99.vb_ref
  12.1 1.2 reshape.100.ob_ref
  13.3 1.2 reshape.101.n2g_ref
  14.6 1.2 reshape.102.n2b_ref
  15.8 1.2 reshape.104.db_ref
  17.0 1.3 reshape.103.ub_ref
  18.3 0.7 dynamic_slice.19
  19.0 1.4 select_reduce_fusion.used_ref
  20.4 102.4 %shard_map.323 = (bf16[2,2048,256]{2,1,0:T(8,128)(2,1)}, bf16[2,2048,256]{2,1,0:T(8,128)(2,1)}, f32[1040,256]{1,0:T(8,128)}, f32[272,1024]{1,0:T(8,128)}, f32[27...) custom-call(s32[1]{0:T(128)} %bitcast.off_ref, bf16[4096,256]{1,0:T(8,128)(2,1)} %x_ref.1, ...), custom_call_target="tpu_custom_call" | custom-call | tf_op jit(solution)/shard_map/pallas_call | solution.py:225
  122.8 0.0 copy-start
  122.8 2.4 dynamic-slice_bitcast_fusion.1
  125.2 3.0 %collective-permute-start = (bf16[2048,256]{1,0:T(8,128)(2,1)}, bf16[2048,256]{1,0:T(8,128)(2,1)}, u32[]{:S(2)}, u32[]{:S(2)}) collective-permute-start(bf16[2048,256]{1,0:T(8,128)(2,1)} %dynamic-slice_bitcast_fusion.1), channel_id=1, source_target_pairs={{0,16},{16,0},{1,17},{17,1},{2,18},{18,2},{3,19},{19,3},{4,20},{20... | collective-permute-start | bytes 3145736 | tf_op jit(solution)/shard_map/ppermute | solution.py:274
  128.2 0.0 copy-done
  128.2 1.0 dynamic-slice_bitcast_fusion
  129.2 0.0 copy-start.3
  129.2 0.0 collective-permute-start.1
  129.3 0.0 all-reduce.3.cloned.1.call-update
  129.3 0.7 copy-done.3
  129.9 88.2 %psum.35 = f32[8,256]{1,0:T(8,128)S(1)} all-reduce(f32[8,256]{1,0:T(8,128)S(1)} %copy-done.3), channel_id=1, replica_groups=mesh['section'=2,'dp'=16] {'section','dp'}, use_global_device_ids=true, to_apply=%region_1.2 | all-reduce | flops 2048 | bytes 16384 | tf_op jit(solution)/shard_map/psum | solution.py:279
  218.2 0.6 fusion.4
  218.7 0.0 collective-permute-done
  218.7 1.7 bitcast_select_fusion.3
  220.4 1.5 maximum_bitcast_fusion
  221.9 0.0 collective-permute-done.1
  221.9 0.1 fusion
  222.0 2.3 maximum_convert_fusion
  224.4 49.4 %all-reduce.3.cloned.1.call-done = (f32[272,768]{1,0:T(8,128)}, f32[272,256]{1,0:T(8,128)}, f32[272,1024]{1,0:T(8,128)}, f32[1040,256]{1,0:T(8,128)}) async-done(((f32[272,768]{1,0:T(8,128)}, f32[272,256]{1,0:T(8,128)}, f32[272,1024]{1,0:T(8,128)}, f32[1040,256]{1,0:T(8,128)}), (f32[272,768]{1,0:T(8,128)}, f32[272,256]{1,0:T(8,128)}, f32[272,1024]{1,0:T(8,128)}, ...) | async-done | bytes 3293200 | tf_op jit(solution)/shard_map/psum | solution.py:279
  273.8 0.0 copy-start.2
  273.8 1.3 slice.68
  275.1 0.0 copy-start.1
  275.1 1.8 slice.67
  276.9 1.3 slice.74
  278.2 2.3 slice.73
  280.4 0.0 copy-done.2
  280.4 0.6 fusion.2
  281.0 0.9 fusion.3
  281.9 0.0 copy-done.1
  281.9 0.6 slice.72
  282.5 1.1 slice.71
Async XLA Ops:
  7.2 266.6 %all-reduce.3.cloned.1.call-start = ((), (), s32[]{:S(2)}) async-start(), calls=%async_computation | async-start | bytes 6586368 | tf_op jit(solution)/shard_map/psum | solution.py:279
  122.8 5.4 %copy-start = (bf16[2,2048,256]{2,1,0:T(8,128)(2,1)S(1)}, bf16[2,2048,256]{2,1,0:T(8,128)(2,1)}, u32[]{:S(2)}) copy-start(bf16[2,2048,256]{2,1,0:T(8,128)(2,1)} %get-tuple-element.25) | copy-start | bytes 6291460
  125.2 93.5 %collective-permute-start = (bf16[2048,256]{1,0:T(8,128)(2,1)}, bf16[2048,256]{1,0:T(8,128)(2,1)}, u32[]{:S(2)}, u32[]{:S(2)}) collective-permute-start(bf16[2048,256]{1,0:T(8,128)(2,1)} %dynamic-slice_bitcast_fusion.1), channel_id=1, source_target_pairs={{0,16},{16,0},{1,17},{17,1},{2,18},{18,2},{3,19},{19,3},{4,20},{20... | collective-permute-start | bytes 3145736 | tf_op jit(solution)/shard_map/ppermute | solution.py:274
  129.2 0.7 copy-start.3
  129.2 92.6 %collective-permute-start.1 = (bf16[2048,256]{1,0:T(8,128)(2,1)}, bf16[2048,256]{1,0:T(8,128)(2,1)S(1)}, u32[]{:S(2)}, u32[]{:S(2)}) collective-permute-start(bf16[2048,256]{1,0:T(8,128)(2,1)} %dynamic-slice_bitcast_fusion), channel_id=1, source_target_pairs={{0,16},{16,0},{1,17},{17,1},{2,18},{18,2},{3,19},{19,3},{4,20},{20... | collective-permute-start | bytes 3145736 | tf_op jit(solution)/shard_map/ppermute | solution.py:274
  273.8 6.6 %copy-start.2 = (f32[272,768]{1,0:T(8,128)S(1)}, f32[272,768]{1,0:T(8,128)}, u32[]{:S(2)}) copy-start(f32[272,768]{1,0:T(8,128)} %get-tuple-element.31) | copy-start | bytes 2506756
  275.1 6.8 %copy-start.1 = (f32[272,1024]{1,0:T(8,128)S(1)}, f32[272,1024]{1,0:T(8,128)}, u32[]{:S(2)}) copy-start(f32[272,1024]{1,0:T(8,128)} %get-tuple-element.33) | copy-start | bytes 3342340
Sparse Core Ops, SparseCore 0:
  129.4 144.3 all-reduce.2

commit v2 on v1

v2 whole, which is shorter than its diff:
```python
import functools
import math

import jax
import jax.numpy as jnp
from jax import lax
from jax.experimental import pallas as pl
from jax.experimental.pallas import tpu as pltpu
from jax.sharding import PartitionSpec as P

BF = jnp.bfloat16
F32 = jnp.float32
SLOTS = 128
HEADS = 8
KEYS = 112
GROUP = 256
EPS = 1e-5


def nn(a, b):
    return lax.dot_general(a, b, (((1,), (0,)), ((), ())), preferred_element_type=F32)


def nt(a, b):
    return lax.dot_general(a, b, (((1,), (1,)), ((), ())), preferred_element_type=F32)


def ln_forward(u, gain, bias, unit_ref, inv_ref, n_ref):
    d = u.shape[0]
    mean = jnp.sum(u, axis=0, keepdims=True) * (1.0 / d)
    c = u - mean
    var = jnp.sum(c * c, axis=0, keepdims=True) * (1.0 / d)
    inv = lax.rsqrt(var + EPS)
    unit = c * inv
    unit_ref[...] = unit
    inv_ref[...] = inv
    n_ref[0:d, :] = (unit * gain + bias).astype(BF)


def lanes2(ref):
    v = ref[...]
    return jnp.concatenate([v, v], axis=1)


def fold(v):
    return v[:, :128] + v[:, 128:]


def ln_backward(gn, unit, inv, gain, gain_acc, bias_acc):
    d = gn.shape[0]
    t = gn * unit
    gain_acc[...] += fold(t)
    bias_acc[...] += fold(gn)
    s = gn * gain
    m1 = jnp.sum(s, axis=0, keepdims=True) * (1.0 / d)
    m2 = jnp.sum(t * gain, axis=0, keepdims=True) * (1.0 / d)
    return inv * (s - m1 - unit * m2)


C0 = math.sqrt(2.0 / math.pi)
C1 = C0 * 0.044715


MESH = pl.DeviceIdType.MESH
PARTS = 3


def plan(dp_bits):
    first = [("dp", 1)]
    turned = [("dp", 2), ("section", 1), ("dp", 4)]
    last = [("dp", 1 << b) for b in range(3, dp_bits)]
    return [first + turned[p:] + turned[:p] + last for p in range(PARTS)]


def kernel(dp_bits, x_hbm, e_hbm, g_hbm, counts_ref, lengths_ref,
           n1g_ref, n1b_ref, wq_ref, qb_ref, wk_ref, wv_ref, vb_ref, wo_ref, ob_ref,
           n2g_ref, n2b_ref, wu_ref, ub_ref, wd_ref, db_ref,
           st_hbm, gr_hbm, sums_ref, vec_ref,
           xv, ev, gv, stS, grS, used_v,
           wqkvT, woT, wuT, wdT, wqkv, vecs, ubv,
           n1T, qkvT, vN, p32, p16, mixT, unit1, inv1, unit2, inv2, n2T, gp, hT,
           bd, ds16, dqkvT, goT, aln, acc, ones_acc, send_buf, recv_buf, vec_send, vec_recv,
           in_sem, local_sem, ex_send, ex_recv, rs_send, rs_recv, ag_send, ag_recv, vs_send, vs_recv):
    D = 256
    FF = 1024
    scale = 32 ** -0.5
    rows = xv.shape[0]
    groups = rows // GROUP
    section = lax.axis_index("section")
    dp = lax.axis_index("dp")
    orders = plan(dp_bits)

    def bit_of(axis, weight):
        return section if axis == "section" else lax.rem(lax.div(dp, weight), 2)

    def across(axis, weight):
        v = bit_of(axis, weight)
        if axis == "section":
            return (1 - section, dp)
        return (section, dp + (1 - 2 * v) * weight)

    barrier = pltpu.get_barrier_semaphore()
    for axis, weight in orders[0]:
        pl.semaphore_signal(barrier, inc=1, device_id=across(axis, weight), device_id_type=MESH)

    def load(g, k):
        src = (x_hbm, e_hbm, g_hbm)[k]
        dst = (xv, ev, gv)[k]
        start = pl.multiple_of(g * GROUP, GROUP)
        return pltpu.make_async_copy(
            src.at[pl.ds(pl.multiple_of(section * rows, GROUP) + start, GROUP), :],
            dst.at[pl.ds(start, GROUP), :], in_sem.at[g, k])

    def start_loads(g, c):
        for k in range(3):
            load(g, k).start()
        return c
    lax.fori_loop(0, groups, start_loads, 0)

    wqkvT[0:256, :] = wq_ref[...].T
    wqkvT[256:512, :] = wk_ref[...].T
    wqkvT[512:768, :] = wv_ref[...].T
    woT[...] = wo_ref[...].T
    wuT[...] = wu_ref[...].T
    wdT[...] = wd_ref[...].T
    wqkv[:, 0:256] = wq_ref[...]
    wqkv[:, 256:512] = wk_ref[...]
    wqkv[:, 512:768] = wv_ref[...]
    for i, r in enumerate((n1g_ref, n1b_ref, qb_ref, vb_ref, ob_ref, n2g_ref, n2b_ref, db_ref)):
        vecs[i] = jnp.broadcast_to(r[...].astype(F32)[None, :], (128, D)).T
    ubv[...] = jnp.broadcast_to(ub_ref[...].astype(F32)[None, :], (128, FF)).T
    acc[...] = jnp.zeros_like(acc)
    ones_acc[...] = jnp.zeros_like(ones_acc)
    aln[...] = jnp.zeros_like(aln)
    bd[...] = jnp.zeros_like(bd)
    ds16[...] = jnp.zeros_like(ds16)
    p16[...] = jnp.zeros_like(p16)
    for it in range(2):
        n1T[it, D:, :] = jnp.ones((16, GROUP), BF)
        mixT[it, D:, :] = jnp.ones((16, GROUP), BF)
        n2T[it, D:, :] = jnp.ones((16, GROUP), BF)
        hT[it, FF:, :] = jnp.ones((16, GROUP), BF)
    prompts = rows // SLOTS
    at_most = lengths_ref.shape[1]
    j_iota = lax.broadcasted_iota(jnp.int32, (1, at_most), 1)
    for p in range(prompts):
        count = counts_ref[section * prompts + p]
        kept = jnp.where(j_iota < count, lengths_ref[pl.ds(section * prompts + p, 1), :], 0)
        total = jnp.sum(kept.astype(F32), axis=1, keepdims=True).astype(jnp.int32)
        used_v[p:p + 1, :] = jnp.broadcast_to(total, (1, 128))

    k_iota = lax.broadcasted_iota(jnp.int32, (KEYS, SLOTS), 0)
    q_iota = lax.broadcasted_iota(jnp.int32, (KEYS, SLOTS), 1)

    def out_copies(g, k):
        stage, out = ((stS, st_hbm), (grS, gr_hbm))[k]
        here = pl.ds(pl.multiple_of(g * GROUP, GROUP), GROUP)
        there = pl.ds(pl.multiple_of(section * rows, GROUP) + pl.multiple_of(g * GROUP, GROUP), GROUP)
        own = pltpu.make_async_copy(stage.at[section, here, :], out.at[there, :], local_sem.at[g, k])
        sent = pltpu.make_async_remote_copy(
            src_ref=stage.at[1 - section, here, :], dst_ref=out.at[there, :],
            send_sem=ex_send.at[g, k], recv_sem=ex_recv.at[g, k],
            device_id=(1 - section, dp), device_id_type=MESH)
        return own, sent

    pl.semaphore_wait(barrier, len(orders[0]))

    def group(g, carry):
        here = pl.ds(pl.multiple_of(g * GROUP, GROUP), GROUP)
        masks = []
        for p in range(2):
            used = used_v[pl.ds(g * 2 + p, 1), :]
            masks.append(jnp.where((k_iota <= q_iota) & (k_iota < used), 0.0, -1e30).astype(F32))

        def forward(u, it):
            ln_forward(u, lanes2(vecs.at[0]), lanes2(vecs.at[1]), unit1.at[it], inv1.at[it], n1T.at[it])
            n1 = n1T[it, 0:D, :]
            qkvT[it, 0:256, :] = (nn(wqkvT[0:256, :], n1) + lanes2(vecs.at[2])).astype(BF)
            qkvT[it, 256:512, :] = nn(wqkvT[256:512, :], n1).astype(BF)
            qkvT[it, 512:768, :] = (nn(wqkvT[512:768, :], n1) + lanes2(vecs.at[3])).astype(BF)
            for p in range(2):
                tok = slice(p * 128, p * 128 + 128)
                kN = qkvT[it, 256:512, tok].T
                vN[it, p] = qkvT[it, 512:768, tok].T
                for h in range(HEADS):
                    bd[p, 32 * h:32 * h + 32, 128 * h:128 * h + 128] = qkvT[it, 32 * h:32 * h + 32, tok]
                for h2 in range(HEADS // 2):
                    sT2 = nn(kN[:KEYS], bd[p, :, 256 * h2:256 * h2 + 256])
                    for hh in range(2):
                        h = h2 * 2 + hh
                        ln = slice(128 * h, 128 * h + 128)
                        s = sT2[:, 128 * hh:128 * hh + 128] + masks[p]
                        m = jnp.max(s, axis=0, keepdims=True)
                        pe = jnp.exp2((s - m) * (scale * math.log2(math.e)))
                        l = jnp.sum(pe, axis=0, keepdims=True)
                        pT = pe * (1.0 / l)
                        p32[it, p, :, ln] = pT
                        p16[it, p, 0:KEYS, ln] = pT.astype(BF)
                        o = nn(qkvT[it, 512 + 32 * h:544 + 32 * h, tok], p16[it, p, :, ln])
                        mixT[it, 32 * h:32 * h + 32, tok] = o.astype(BF)
            middle = u + nn(woT[...], mixT[it, 0:D, :]) + lanes2(vecs.at[4])
            ln_forward(middle, lanes2(vecs.at[5]), lanes2(vecs.at[6]), unit2.at[it], inv2.at[it], n2T.at[it])
            n2 = n2T[it, 0:D, :]
            for c in range(FF // 128):
                rows = slice(c * 128, c * 128 + 128)
                v = nn(wuT[rows, :], n2) + lanes2(ubv.at[rows])
                v2 = v * v
                t = jnp.tanh(v * (C0 + C1 * v2))
                h1 = 0.5 + 0.5 * t
                hid = v * h1
                gp[it, rows, :] = h1 + (hid - hid * h1) * (2.0 * C0 + 6.0 * C1 * v2)
                hT[it, rows, :] = hid.astype(BF)
            return middle + nn(wdT[...], hT[it, 0:FF, :]) + lanes2(vecs.at[7])

        def backward(g, it):
            low = g.astype(BF)
            t = nt(hT[it], low)
            acc[0:FF, :] += t[0:FF]
            ones_acc[0] += t[FF:]
            for c in range(FF // 128):
                rows = slice(c * 128, c * 128 + 128)
                dh = nn(wd_ref[rows, :], low)
                goT[rows, :] = (dh * gp[it, rows, :]).astype(BF)
            dpre = goT[...]
            for j in range(FF // D):
                t = nt(n2T[it], goT[j * D:j * D + D, :])
                acc[FF + j * D:FF + j * D + D, :] += t[0:D]
                ones_acc[1 + j] += t[D:]
            dn2 = nn(wu_ref[...], dpre)
            dmid = g + ln_backward(dn2, unit2[it], inv2[it], lanes2(vecs.at[5]), aln.at[2], aln.at[3])
            alow = dmid.astype(BF)
            t = nt(mixT[it], alow)
            acc[2 * FF + 3 * D:2 * FF + 4 * D, :] += t[0:D]
            ones_acc[8] += t[D:]
            dmix = nn(wo_ref[...], alow).astype(BF)
            for p in range(2):
                tok = slice(p * 128, p * 128 + 128)
                for h in range(HEADS):
                    bd[p, 32 * h:32 * h + 32, 128 * h:128 * h + 128] = dmix[32 * h:32 * h + 32, tok]
                for h2 in range(HEADS // 2):
                    dp2 = nn(vN[it, p, 0:KEYS, :], bd[p, :, 256 * h2:256 * h2 + 256])
                    for hh in range(2):
                        h = h2 * 2 + hh
                        ln = slice(128 * h, 128 * h + 128)
                        hr = slice(32 * h, 32 * h + 32)
                        pT = p32[it, p, :, ln]
                        t = pT * dp2[:, 128 * hh:128 * hh + 128]
                        dsum = jnp.sum(t, axis=0, keepdims=True)
                        ds16[p, 0:KEYS, ln] = (t - pT * dsum).astype(BF)
                        ds = ds16[p, :, ln]
                        dqkvT[32 * h:32 * h + 32, tok] = (nn(qkvT[it, 256 + 32 * h:288 + 32 * h, tok], ds) * scale).astype(BF)
                        dqkvT[256 + 32 * h:288 + 32 * h, tok] = (nt(qkvT[it, hr, tok], ds) * scale).astype(BF)
                        dqkvT[512 + 32 * h:544 + 32 * h, tok] = nt(dmix[hr, tok], p16[it, p, :, ln]).astype(BF)
            dqkv = dqkvT[...]
            for j in range(3):
                t = nt(n1T[it], dqkvT[j * D:j * D + D, :])
                acc[2 * FF + j * D:2 * FF + j * D + D, :] += t[0:D]
                ones_acc[5 + j] += t[D:]
            dn1 = nn(wqkv[...], dqkv)
            return dmid + ln_backward(dn1, unit1[it], inv1[it], lanes2(vecs.at[0]), aln.at[0], aln.at[1])


        for k in range(3):
            load(g, k).wait()
        eT = ev[here, :].T.astype(F32)
        u1 = xv[here, :].T.astype(F32) + eT
        s1 = forward(u1, 0).astype(BF)
        stS[0, here, :] = s1.T
        u2 = s1.astype(F32) + eT
        s2 = forward(u2, 1).astype(BF)
        stS[1, here, :] = s2.T
        for c in out_copies(g, 0):
            c.start()
        g2 = backward(gv[here, :].T.astype(F32), 1)
        g2l = g2.astype(BF)
        grS[1, here, :] = g2l.T
        g1 = backward(g2l.astype(F32), 0)
        grS[0, here, :] = g1.astype(BF).T
        for c in out_copies(g, 1):
            c.start()
        return carry

    lax.fori_loop(0, groups, group, 0)

    for i, j in enumerate((0, 1, 5, 6)):
        vec_ref[j:j + 1, :] = jnp.sum(aln[i].T, axis=0, keepdims=True)
    for i, j in ((0, 7), (1, 8), (2, 9), (3, 10), (4, 11), (5, 2), (7, 3), (8, 4)):
        vec_ref[j:j + 1, :] = ones_acc[i, 0:1, :]
    vec_ref[12:16, :] = jnp.zeros((4, D), F32)

    total_rows = acc.shape[0]
    part_rows = total_rows // PARTS
    offs = [p * part_rows for p in range(PARTS)]
    sizes = [part_rows] * PARTS
    pending = [None] * PARTS
    history = [[] for _ in range(PARTS)]
    used_rows = 0
    vec_pending = None

    def finish_vec():
        nonlocal vec_pending
        if vec_pending is not None:
            copy, s = vec_pending
            copy.wait()
            vec_ref[...] = vec_ref[...] + vec_recv[s]
            vec_pending = None

    for s in range(len(orders[0])):
        for p in range(PARTS):
            if pending[p] is not None:
                pending[p]()
            axis, weight = orders[p][s]
            v = bit_of(axis, weight)
            off, size = offs[p], sizes[p]
            halve = size >= 32
            n = size // 2 if halve else size
            src_off = pl.multiple_of(off + (1 - v) * n, 16) if halve else off
            keep = pl.multiple_of(off + v * n, 16) if halve else off
            region = pl.ds(used_rows, n)
            used_rows += n
            send_buf[region, :] = acc[pl.ds(src_off, n), :].astype(BF)
            copy = pltpu.make_async_remote_copy(
                src_ref=send_buf.at[region, :], dst_ref=recv_buf.at[region, :],
                send_sem=rs_send.at[s, p], recv_sem=rs_recv.at[s, p],
                device_id=across(axis, weight), device_id_type=MESH)
            copy.start()

            def finish(copy=copy, keep=keep, n=n, region=region, halve=halve):
                copy.wait()
                own = acc[pl.ds(keep, n), :]
                if not halve:
                    own = own.astype(BF).astype(F32)
                acc[pl.ds(keep, n), :] = own + recv_buf[region, :].astype(F32)
            pending[p] = finish
            if halve:
                history[p].append((axis, weight, off, n, keep))
                offs[p], sizes[p] = keep, n
        finish_vec()
        axis, weight = orders[0][s]
        vec_send[s] = vec_ref[...]
        copy = pltpu.make_async_remote_copy(
            src_ref=vec_send.at[s], dst_ref=vec_recv.at[s],
            send_sem=vs_send.at[s], recv_sem=vs_recv.at[s],
            device_id=across(axis, weight), device_id_type=MESH)
        copy.start()
        vec_pending = (copy, s)
    finish_vec()
    for p in range(PARTS):
        pending[p]()
        sums_ref[pl.ds(offs[p], sizes[p]), :] = acc[pl.ds(offs[p], sizes[p]), :].astype(BF)
    last = [None] * PARTS
    for s in range(max(len(h) for h in history)):
        for p in range(PARTS):
            if last[p] is not None:
                last[p].wait()
            axis, weight, off, n, keep = history[p][-1 - s]
            copy = pltpu.make_async_remote_copy(
                src_ref=sums_ref.at[pl.ds(keep, n), :], dst_ref=sums_ref.at[pl.ds(keep, n), :],
                send_sem=ag_send.at[s, p], recv_sem=ag_recv.at[s, p],
                device_id=across(axis, weight), device_id_type=MESH)
            copy.start()
            last[p] = copy
    for p in range(PARTS):
        last[p].wait()

    def finish_out(g, c):
        for k in range(2):
            own, sent = out_copies(g, k)
            own.wait()
            sent.wait()
        return c
    lax.fori_loop(0, groups, finish_out, 0)


def compute(x, e, g, counts, lengths, params, dp_size):
    local = x.shape[0]
    rows = local // 2
    groups = rows // GROUP
    dp_bits = dp_size.bit_length() - 1
    stages = dp_bits + 1
    hbm = pl.BlockSpec(memory_space=pl.ANY)
    smem = pl.BlockSpec(memory_space=pltpu.SMEM)
    vmem = pl.BlockSpec(memory_space=pltpu.VMEM)
    outs = [
        jax.ShapeDtypeStruct((local, 256), BF),
        jax.ShapeDtypeStruct((local, 256), BF),
        jax.ShapeDtypeStruct((3072, 256), BF),
        jax.ShapeDtypeStruct((16, 256), F32),
    ]
    buf_rows = 0
    size = 3072 // PARTS
    for _ in range(stages):
        n = size // 2 if size >= 32 else size
        buf_rows += n * PARTS
        size = n
    return pl.pallas_call(
        functools.partial(kernel, dp_bits),
        out_shape=outs,
        in_specs=[hbm, hbm, hbm, smem, vmem] + [vmem] * 15,
        out_specs=[hbm, hbm, vmem, vmem],
        scratch_shapes=[
            pltpu.VMEM((rows, 256), BF), pltpu.VMEM((rows, 256), BF), pltpu.VMEM((rows, 256), BF),
            pltpu.VMEM((2, rows, 256), BF), pltpu.VMEM((2, rows, 256), BF),
            pltpu.VMEM((rows // SLOTS, 128), jnp.int32),
            pltpu.VMEM((768, 256), BF), pltpu.VMEM((256, 256), BF), pltpu.VMEM((1024, 256), BF),
            pltpu.VMEM((256, 1024), BF), pltpu.VMEM((256, 768), BF),
            pltpu.VMEM((8, 256, 128), F32), pltpu.VMEM((1024, 128), F32),
            pltpu.VMEM((2, 272, GROUP), BF),
            pltpu.VMEM((2, 768, GROUP), BF),
            pltpu.VMEM((2, 2, 128, 256), BF),
            pltpu.VMEM((2, 2, KEYS, 1024), F32),
            pltpu.VMEM((2, 2, 128, 1024), BF),
            pltpu.VMEM((2, 272, GROUP), BF),
            pltpu.VMEM((2, 256, GROUP), F32), pltpu.VMEM((2, 1, GROUP), F32),
            pltpu.VMEM((2, 256, GROUP), F32), pltpu.VMEM((2, 1, GROUP), F32),
            pltpu.VMEM((2, 272, GROUP), BF),
            pltpu.VMEM((2, 1024, GROUP), F32),
            pltpu.VMEM((2, 1040, GROUP), BF),
            pltpu.VMEM((2, 256, 1024), BF),
            pltpu.VMEM((2, 128, 1024), BF),
            pltpu.VMEM((768, GROUP), BF),
            pltpu.VMEM((1024, GROUP), BF),
            pltpu.VMEM((4, 256, 128), F32),
            pltpu.VMEM((3072, 256), F32),
            pltpu.VMEM((9, 16, 256), F32),
            pltpu.VMEM((buf_rows, 256), BF), pltpu.VMEM((buf_rows, 256), BF),
            pltpu.VMEM((stages, 16, 256), F32), pltpu.VMEM((stages, 16, 256), F32),
            pltpu.SemaphoreType.DMA((groups, 3)),
            pltpu.SemaphoreType.DMA((groups, 2)),
            pltpu.SemaphoreType.DMA((groups, 2)),
            pltpu.SemaphoreType.DMA((groups, 2)),
            pltpu.SemaphoreType.DMA((stages, PARTS)),
            pltpu.SemaphoreType.DMA((stages, PARTS)),
            pltpu.SemaphoreType.DMA((stages, PARTS)),
            pltpu.SemaphoreType.DMA((stages, PARTS)),
            pltpu.SemaphoreType.DMA((stages,)),
            pltpu.SemaphoreType.DMA((stages,)),
        ],
        compiler_params=pltpu.CompilerParams(
            vmem_limit_bytes=56 * 1024 * 1024, collective_id=0, has_side_effects=True),
    )(x, e, g, counts, lengths, *params)


def widen_kernel(st_ref, gr_ref, sums_ref, vec_ref, st_out, gr_out, n1g, n1b, wq, qb, wk, wv, vb, wo, ob, n2g, n2b, wu, ub, wd, db):
    st_out[0] = st_ref[...]
    gr_out[0] = gr_ref[...].astype(F32)

    @pl.when(pl.program_id(0) == 0)
    def _():
        wd[...] = sums_ref[0:1024, :].astype(F32)
        for j in range(4):
            wu[:, 256 * j:256 * j + 256] = sums_ref[1024 + 256 * j:1280 + 256 * j, :].astype(F32)
            ub[256 * j:256 * j + 256] = vec_ref[8 + j]
        for j, r in enumerate((wq, wk, wv, wo)):
            r[...] = sums_ref[2048 + 256 * j:2304 + 256 * j, :].astype(F32)
        for j, r in enumerate((n1g, n1b, qb, vb, ob, n2g, n2b, db)):
            r[...] = vec_ref[j]


def widen(st, gr, sums, vec, params):
    local = st.shape[0]
    block = min(512, local)
    full = lambda a: pl.BlockSpec(a.shape, lambda i: (0,) * a.ndim)
    outs = [jax.ShapeDtypeStruct((1, local, 256), BF), jax.ShapeDtypeStruct((1, local, 256), F32)]
    outs += [jax.ShapeDtypeStruct(p.shape, F32) for p in params]
    blk = pl.BlockSpec((block, 256), lambda i: (i, 0))
    oblk = pl.BlockSpec((1, block, 256), lambda i: (0, i, 0))
    return pl.pallas_call(
        widen_kernel,
        grid=(local // block,),
        out_shape=outs,
        in_specs=[blk, blk, full(sums), full(vec)],
        out_specs=[oblk, oblk] + [full(o) for o in outs[2:]],
        compiler_params=pltpu.CompilerParams(vmem_limit_bytes=40 * 1024 * 1024),
    )(st, gr, sums, vec)


def solution(mesh):
    dp_size = mesh.shape["dp"]

    def body(x, e, g, counts, lengths, *params):
        st, gr, sums, vec = compute(x, e, g, counts, lengths, params, dp_size)
        return tuple(widen(st, gr, sums, vec, params))

    placed = (P("dp", None),) * 3 + (P("dp"), P("dp", None)) + (P(),) * 15
    return jax.shard_map(
        body,
        mesh=mesh,
        in_specs=placed,
        out_specs=(P("section", "dp", None),) * 2 + (P(),) * 15,
        check_vma=False,
    )
```

time: 291 us -> 154 us (0.53)
  blocking collectives: 88.2 us -> 0 us
  waiting for transfers between devices: 49.5 us -> 0 us
  Pallas kernels: 102 us -> 147 us
  local copies, waits for them, and re-layouts: 26.2 us -> 5.3 us
  between operations: 14.1 us -> 0.68 us
  other arithmetic: 7.01 us -> 0 us
  starting transfers between devices: 3.01 us -> 0 us
    psum x1 -> x0, blocking collectives: 88.2 us -> none  [body(): lax.psum((awd, awu, awqkv, awo, aln), ('section', 'dp'))]
    psum x1 -> x0, waiting for transfers between devices: 49.4 us -> none  [body(): lax.psum((awd, awu, awqkv, awo, aln), ('section', 'dp'))]
    pallas_call x1 -> x2, Pallas kernels: 102 us -> 147 us  [the longest x1 142 us: compute(): pl.pallas_call(functools.partial(kernel, dp_bits), out_shape=outs, in_spe...]
    reshape x9 -> x0, local copies, waits for them, and re-layouts: 11 us -> none  [compute(): row = lambda v: v.reshape(1, -1)]
    slice x9 -> x0, local copies, waits for them, and re-layouts: 10.3 us -> none  [the longest x1 2.26 us: body(): awd[:1024]]
    unnamed x8, local copies, waits for them, and re-layouts: 0.68 us -> 5.3 us
    squeeze x2 -> x0, local copies, waits for them, and re-layouts: 3.45 us -> none  [exchange(): other = lax.dynamic_index_in_dim(pair, 1 - section, 0, keepdims=False)]
    ppermute x2 -> x0, starting transfers between devices: 2.97 us -> none  [exchange(): got = lax.ppermute(other, 'section', [(0, 1), (1, 0)])]
  transfers between devices with their start and end apart: 3 -> 0, of which waited for: 1 -> 0; matrix products, arithmetic and copies ran while one was open for 2% -> 0% of each run, Pallas kernels for 0% -> 0%
where the time goes in v2:
time: 154 us; the launch traced here: 153 us
  Pallas kernels  147 us (95%)
  local copies, waits for them, and re-layouts  5.3 us (3%)
    pallas_call x1, Pallas kernels, compute(): pl.pallas_call(functools.partial(kernel, dp_bits), out_shape=outs, in_spe...  142 us
    unnamed x8, local copies, waits for them, and re-layouts  5.3 us
    pallas_call x1, Pallas kernels, widen(): pl.pallas_call(widen_kernel, grid=(local // block,), out_shape=outs, in_s...  5.2 us

profile of v2, /device:TPU:0, one launch (start us, length us, event | category | flops | bytes accessed | tf_op | source)
XLA Modules:
  0.0 153.3 jit_solution(8754176956792180942)
XLA Ops:
  0.7 142.1 %shard_map.323 = (bf16[4096,256]{1,0:T(8,128)(2,1)}, bf16[4096,256]{1,0:T(8,128)(2,1)}, bf16[3072,256]{1,0:T(8,128)(2,1)}, f32[16,256]{1,0:T(8,128)}) custom-call(bf16[4096,256]{1,0:T(8,128)(2,1)} %x_hbm.1, bf16[4096,256]{1,0:T(8,128)(2,1)} %e_hbm.1, bf16[4096,256]{1,0:T(8,128)(2,1)} %g_hbm.1, s32[32]{0:T(128)} %counts_ref.1, s32[32,50]{1,0:T(8,128)} %lengths_ref.1, ...), custom_call_target="tpu_custom_call" | custom-call | tf_op jit(solution)/shard_map/pallas_call | solution.py:396
  142.8 0.0 copy-start
  142.8 1.6 %copy-done = bf16[4096,256]{1,0:T(8,128)(2,1)S(1)} copy-done((bf16[4096,256]{1,0:T(8,128)(2,1)S(1)}, bf16[4096,256]{1,0:T(8,128)(2,1)}, u32[]{:S(2)}) %copy-start) | copy-done | bytes 2097176
  144.4 0.0 copy-start.1
  144.4 1.6 %copy-done.1 = bf16[4096,256]{1,0:T(8,128)(2,1)S(1)} copy-done((bf16[4096,256]{1,0:T(8,128)(2,1)S(1)}, bf16[4096,256]{1,0:T(8,128)(2,1)}, u32[]{:S(2)}) %copy-start.1) | copy-done | bytes 2097176
  145.9 0.0 copy-start.2
  145.9 1.4 copy-done.2
  147.4 0.0 copy-start.3
  147.4 0.7 copy-done.3
  148.1 5.2 %shard_map.324 = (bf16[1,4096,256]{2,1,0:T(8,128)(2,1)}, f32[1,4096,256]{2,1,0:T(8,128)}, f32[256]{0:T(256)}, f32[256]{0:T(256)}, f32[256,256]{1,0:T(8,128)}, /*...) custom-call(bf16[4096,256]{1,0:T(8,128)(2,1)S(1)} %copy-done, ...), custom_call_target="tpu_custom_call" | custom-call | tf_op jit(solution)/shard_map/pallas_call | solution.py:468
Async XLA Ops:
  142.8 1.6 %copy-start = (bf16[4096,256]{1,0:T(8,128)(2,1)S(1)}, bf16[4096,256]{1,0:T(8,128)(2,1)}, u32[]{:S(2)}) copy-start(bf16[4096,256]{1,0:T(8,128)(2,1)} %get-tuple-element.21.st_ref) | copy-start | bytes 6291460
  144.4 1.6 %copy-start.1 = (bf16[4096,256]{1,0:T(8,128)(2,1)S(1)}, bf16[4096,256]{1,0:T(8,128)(2,1)}, u32[]{:S(2)}) copy-start(bf16[4096,256]{1,0:T(8,128)(2,1)} %get-tuple-element.22.gr_ref) | copy-start | bytes 6291460
  145.9 1.4 copy-start.2
  147.4 0.7 copy-start.3

commit v3 on v2

v3 whole, which is shorter than its diff:
```python
import functools
import math

import jax
import jax.numpy as jnp
from jax import lax
from jax.experimental import pallas as pl
from jax.experimental.pallas import tpu as pltpu
from jax.sharding import PartitionSpec as P

BF = jnp.bfloat16
F32 = jnp.float32
SLOTS = 128
HEADS = 8
KEYS = 112
GROUP = 512
CH = 256
PG = GROUP // SLOTS
EPS = 1e-5


def nn(a, b):
    return lax.dot_general(a, b, (((1,), (0,)), ((), ())), preferred_element_type=F32)


def nt(a, b):
    return lax.dot_general(a, b, (((1,), (1,)), ((), ())), preferred_element_type=F32)


C0 = math.sqrt(2.0 / math.pi)
C1 = C0 * 0.044715
SCALE = 32 ** -0.5
D = 256
FF = 1024


def ln_forward(u_ref, gain, bias, unit_ref, inv_ref, n_ref, lanes):
    for b in range(lanes.start, lanes.stop, 128):
        ln = slice(b, b + 128)
        u = u_ref[:, ln]
        mean = jnp.sum(u, axis=0, keepdims=True) * (1.0 / D)
        c = u - mean
        var = jnp.sum(c * c, axis=0, keepdims=True) * (1.0 / D)
        inv = lax.rsqrt(var + EPS)
        unit = c * inv
        unit_ref[:, ln] = unit
        inv_ref[:, ln] = inv
        n_ref[0:D, ln] = (unit * gain[...] + bias[...]).astype(BF)


def ln_backward(gn_ref, res_ref, unit_ref, inv_ref, gain, gain_acc, bias_acc, out_ref, low_ref, lanes):
    for b in range(lanes.start, lanes.stop, 128):
        ln = slice(b, b + 128)
        gn = gn_ref[:, ln]
        unit = unit_ref[:, ln]
        t = gn * unit
        gain_acc[...] += t
        bias_acc[...] += gn
        s = gn * gain[...]
        m1 = jnp.sum(s, axis=0, keepdims=True) * (1.0 / D)
        m2 = jnp.sum(t * gain[...], axis=0, keepdims=True) * (1.0 / D)
        out = res_ref[:, ln] + inv_ref[:, ln] * (s - m1 - unit * m2)
        out_ref[:, ln] = out
        low_ref[:, ln] = out.astype(BF)


class Refs:
    pass


def chain(R, c, masks):
    L = slice(c * CH, c * CH + CH)
    prompts = range(c * CH // SLOTS, (c + 1) * CH // SLOTS)
    R.load(c)
    yield
    for it in range(2):
        ln_forward(R.uT, R.vecs.at[0], R.vecs.at[1], R.unit1.at[it], R.inv1.at[it], R.n1T.at[it], L)
        yield
        n1 = R.n1T[it, 0:D, L]
        for j, vec in ((0, 2), (1, None), (2, 3)):
            rows = slice(256 * j, 256 * j + 256)
            y = nn(R.wqkvT[rows, :], n1)
            if vec is not None:
                v = R.vecs[vec]
                y = y + jnp.concatenate([v] * (CH // 128), axis=1)
            R.qkvT[it, rows, L] = y.astype(BF)
        yield
        for p in prompts:
            tok = slice(p * 128, p * 128 + 128)
            for h in range(HEADS):
                R.bdq[p, h // 2, 32 * (h % 4):32 * (h % 4) + 32, 128 * (h % 2):128 * (h % 2) + 128] = R.qkvT[it, 32 * h:32 * h + 32, tok]
            R.kN[p] = R.qkvT[it, 256:512, tok].T
            for h2 in range(HEADS // 2):
                R.sc[p, :, 256 * h2:256 * h2 + 256] = nn(R.kN[p, 0:KEYS, 128 * (h2 // 2):128 * (h2 // 2) + 128], R.bdq[p, h2])
            R.vN[it, p] = R.qkvT[it, 512:768, tok].T
            yield
        for p in prompts:
            tok = slice(p * 128, p * 128 + 128)
            for h in range(HEADS):
                ln = slice(128 * h, 128 * h + 128)
                s = R.sc[p, :, ln] + masks[p]
                m = jnp.max(s, axis=0, keepdims=True)
                pe = jnp.exp2((s - m) * (SCALE * math.log2(math.e)))
                l = jnp.sum(pe, axis=0, keepdims=True)
                pT = pe * (1.0 / l)
                R.p32[it, p, :, ln] = pT
                R.p16[it, p, 0:KEYS, ln] = pT.astype(BF)
            yield
            for h2 in range(HEADS // 2):
                ln = slice(256 * h2, 256 * h2 + 256)
                o = nn(R.qkvT[it, 512 + 64 * h2:576 + 64 * h2, tok], R.p16[it, p, :, ln])
                R.mixT[it, 64 * h2:64 * h2 + 32, tok] = o[0:32, 0:128].astype(BF)
                R.mixT[it, 64 * h2 + 32:64 * h2 + 64, tok] = o[32:64, 128:256].astype(BF)
            yield
        y = nn(R.woT[...], R.mixT[it, 0:D, L])
        for b in range(L.start, L.stop, 128):
            R.mid[:, b:b + 128] = R.uT[:, b:b + 128] + R.vecs[4] + y[:, b - L.start:b - L.start + 128]
        yield
        for p in prompts:
            for h in range(HEADS):
                ln = slice(128 * h, 128 * h + 128)
                R.pN[it, p, :, ln] = R.p16[it, p, :, ln].T
        ln_forward(R.mid, R.vecs.at[5], R.vecs.at[6], R.unit2.at[it], R.inv2.at[it], R.n2T.at[it], L)
        yield
        n2 = R.n2T[it, 0:D, L]
        for half in range(2):
            rows = slice(512 * half, 512 * half + 512)
            R.pre[rows, L] = nn(R.wuT[rows, :], n2)
            yield
            for r in range(rows.start, rows.stop, 32):
                for b in range(L.start, L.stop, 128):
                    at = (slice(r, r + 32), slice(b, b + 128))
                    v = R.pre[at] + R.ubv[r:r + 32, :]
                    v2 = v * v
                    t = jnp.tanh(v * (C0 + C1 * v2))
                    h1 = 0.5 + 0.5 * t
                    hid = v * h1
                    R.gp[it, r:r + 32, b:b + 128] = h1 + (hid - hid * h1) * (2.0 * C0 + 6.0 * C1 * v2)
                    R.hT[it, r:r + 32, b:b + 128] = hid.astype(BF)
            yield
        y = nn(R.wdT[...], R.hT[it, 0:FF, L])
        for b in range(L.start, L.stop, 128):
            out = R.mid[:, b:b + 128] + R.vecs[7] + y[:, b - L.start:b - L.start + 128]
            R.finish_forward(it, b, out.astype(BF))
        if it == 1:
            R.send(c, 0)
        yield
    for it in (1, 0):
        for half in range(2):
            rows = slice(512 * half, 512 * half + 512)
            R.pre[rows, L] = nn(R.wd_ref[rows, :], R.lowT[it, :, L])
            yield
            for r in range(rows.start, rows.stop, 32):
                for b in range(L.start, L.stop, 128):
                    at = (slice(r, r + 32), slice(b, b + 128))
                    R.dpre[it, r:r + 32, b:b + 128] = (R.pre[at] * R.gp[it, r:r + 32, b:b + 128]).astype(BF)
            yield
        R.dn[:, L] = nn(R.wu_ref[...], R.dpre[it, :, L])
        yield
        ln_backward(R.dn, R.gT, R.unit2.at[it], R.inv2.at[it], R.vecs.at[5], R.aln.at[2], R.aln.at[3], R.gT, R.alow.at[it], L)
        yield
        R.dmixT[:, L] = nn(R.wo_ref[...], R.alow[it, :, L]).astype(BF)
        yield
        for p in prompts:
            tok = slice(p * 128, p * 128 + 128)
            for h in range(HEADS):
                R.bdo[p, h // 2, 32 * (h % 4):32 * (h % 4) + 32, 128 * (h % 2):128 * (h % 2) + 128] = R.dmixT[32 * h:32 * h + 32, tok]
            for h2 in range(HEADS // 2):
                R.sc[p, :, 256 * h2:256 * h2 + 256] = nn(R.vN[it, p, 0:KEYS, 128 * (h2 // 2):128 * (h2 // 2) + 128], R.bdo[p, h2])
            yield
        for p in prompts:
            tok = slice(p * 128, p * 128 + 128)
            for h in range(HEADS):
                ln = slice(128 * h, 128 * h + 128)
                pT = R.p32[it, p, :, ln]
                t = pT * R.sc[p, :, ln]
                dsum = jnp.sum(t, axis=0, keepdims=True)
                R.ds16[p, 0:KEYS, ln] = (t - pT * dsum).astype(BF)
                R.dsN[p, :, ln] = R.ds16[p, :, ln].T
            yield
            for h2 in range(HEADS // 2):
                r = 64 * h2
                ln = slice(256 * h2, 256 * h2 + 256)
                for base, left, right, scaled in (
                    (512, R.dmixT[r:r + 64, tok], R.pN[it, p, :, ln], None),
                    (0, R.qkvT[it, 256 + r:320 + r, tok], R.ds16[p, :, ln], SCALE),
                    (256, R.qkvT[it, r:r + 64, tok], R.dsN[p, :, ln], SCALE)):
                    d = nn(left, right)
                    top, low = d[0:32, 0:128], d[32:64, 128:256]
                    if scaled is not None:
                        top, low = top * scaled, low * scaled
                    R.dqkvT[it, base + r:base + r + 32, tok] = top.astype(BF)
                    R.dqkvT[it, base + r + 32:base + r + 64, tok] = low.astype(BF)
            yield
        R.dn[:, L] = nn(R.wqkv[...], R.dqkvT[it, :, L])
        yield
        ln_backward(R.dn, R.gT, R.unit1.at[it], R.inv1.at[it], R.vecs.at[0], R.aln.at[0], R.aln.at[1], R.gT, R.gl16, L)
        for b in range(L.start, L.stop, 128):
            R.finish_backward(it, b, R.gl16[:, b:b + 128])
        if it == 0:
            R.send(c, 1)
        yield


def weight_terms(R, it):
    for i in range(0, FF, 256):
        stop = i + 256 if i + 256 < FF else FF + 16
        R.add_wd(i, nt(R.hT[it, i:stop, :], R.lowT[it]))
        yield
    for j in range(FF // D):
        R.add_wu(j, nt(R.n2T[it], R.dpre[it, j * D:j * D + D, :]))
        yield
    R.add_wo(nt(R.mixT[it], R.alow[it]))
    yield
    for j in range(3):
        R.add_wqkv(j, nt(R.n1T[it], R.dqkvT[it, j * D:j * D + D, :]))
        yield


def run_group(R, masks, lag):
    chains = [chain(R, c, masks) for c in range(GROUP // CH)]
    counts = [0] * len(chains)
    done = [False] * len(chains)
    terms = []
    started = set()
    while not all(done) or terms:
        for i, ch in enumerate(chains):
            if done[i] or (i > 0 and counts[i] + lag > counts[i - 1] and not done[i - 1]):
                continue
            try:
                next(ch)
                counts[i] += 1
            except StopIteration:
                done[i] = True
        if min(counts) >= R.bwd1_done and 1 not in started:
            started.add(1)
            terms.append(weight_terms(R, 1))
        if all(done) and 0 not in started:
            started.add(0)
            terms.append(weight_terms(R, 0))
        for t in list(terms):
            try:
                next(t)
            except StopIteration:
                terms.remove(t)


SCRATCH = dict(
    wqkvT=((768, 256), BF), woT=((256, 256), BF), wuT=((1024, 256), BF), wdT=((256, 1024), BF), wqkv=((256, 768), BF),
    vecs=((8, 256, 128), F32), ubv=((1024, 128), F32),
    n1T=((2, 272, GROUP), BF), qkvT=((2, 768, GROUP), BF), kN=((PG, 128, 256), BF), vN=((2, PG, 128, 256), BF),
    bdq=((PG, 4, 128, 256), BF), bdo=((PG, 4, 128, 256), BF),
    sc=((PG, KEYS, 1024), F32), p32=((2, PG, KEYS, 1024), F32), p16=((2, PG, 128, 1024), BF), pN=((2, PG, 128, 1024), BF),
    ds16=((PG, 128, 1024), BF), dsN=((PG, 128, 1024), BF),
    mixT=((2, 272, GROUP), BF), uT=((256, GROUP), F32), eT=((256, GROUP), BF), mid=((256, GROUP), F32), gT=((256, GROUP), F32), dn=((256, GROUP), F32),
    gl16=((256, GROUP), BF),
    unit1=((2, 256, GROUP), F32), inv1=((2, 1, GROUP), F32), unit2=((2, 256, GROUP), F32), inv2=((2, 1, GROUP), F32),
    n2T=((2, 272, GROUP), BF), pre=((1024, GROUP), F32), gp=((2, 1024, GROUP), F32), hT=((2, 1040, GROUP), BF),
    lowT=((2, 256, GROUP), BF), dpre=((2, 1024, GROUP), BF), alow=((2, 256, GROUP), BF), dmixT=((256, GROUP), BF),
    dqkvT=((2, 768, GROUP), BF), aln=((4, 256, 128), F32))


def prologue(R, n1g, n1b, wq, qb, wk, wv, vb, wo, ob, n2g, n2b, wu, ub, wd, db):
    R.wqkvT[0:256, :] = wq[...].T
    R.wqkvT[256:512, :] = wk[...].T
    R.wqkvT[512:768, :] = wv[...].T
    R.woT[...] = wo[...].T
    R.wuT[...] = wu[...].T
    R.wdT[...] = wd[...].T
    R.wqkv[:, 0:256] = wq[...]
    R.wqkv[:, 256:512] = wk[...]
    R.wqkv[:, 512:768] = wv[...]
    for i, r in enumerate((n1g, n1b, qb, vb, ob, n2g, n2b, db)):
        R.vecs[i] = jnp.broadcast_to(r[...].astype(F32).reshape(1, D), (128, D)).T
    R.ubv[...] = jnp.broadcast_to(ub[...].astype(F32).reshape(1, FF), (128, FF)).T
    for r in (R.aln, R.bdq, R.bdo, R.ds16, R.p16):
        r[...] = jnp.zeros_like(r)
    for it in range(2):
        for r in (R.n1T, R.mixT, R.n2T):
            r[it, D:, :] = jnp.ones((16, GROUP), BF)
        R.hT[it, FF:, :] = jnp.ones((16, GROUP), BF)


LAG = 3
MESH = pl.DeviceIdType.MESH
PARTS = 3


def plan(dp_bits):
    first = [("dp", 1)]
    turned = [("dp", 2), ("section", 1), ("dp", 4)]
    last = [("dp", 1 << b) for b in range(3, dp_bits)]
    return [first + turned[p:] + turned[:p] + last for p in range(PARTS)]


def comm_scratch(rows, buf_rows, stages):
    blocks = rows // CH
    dma = pltpu.SemaphoreType.DMA
    return dict(
        xv=pltpu.VMEM((rows, 256), BF), ev=pltpu.VMEM((rows, 256), BF), gv=pltpu.VMEM((rows, 256), BF),
        stS=pltpu.VMEM((2, rows, 256), BF), grS=pltpu.VMEM((2, rows, 256), BF),
        used_v=pltpu.VMEM((rows // SLOTS, 128), jnp.int32),
        acc=pltpu.VMEM((3072, 256), F32), ones_acc=pltpu.VMEM((9, 16, 256), F32),
        send_buf=pltpu.VMEM((buf_rows, 256), BF), recv_buf=pltpu.VMEM((buf_rows, 256), BF),
        vec_send=pltpu.VMEM((stages, 16, 256), F32), vec_recv=pltpu.VMEM((stages, 16, 256), F32),
        in_sem=dma((blocks, 3)), local_sem=dma((blocks, 2)), ex_send=dma((blocks, 2)), ex_recv=dma((blocks, 2)),
        rs_send=dma((stages, PARTS)), rs_recv=dma((stages, PARTS)), ag_send=dma((stages, PARTS)), ag_recv=dma((stages, PARTS)),
        vs_send=dma((stages,)), vs_recv=dma((stages,)))


def kernel(dp_bits, x_hbm, e_hbm, g_hbm, counts_ref, lengths_ref, *refs):
    ws = refs[:15]
    st_hbm, gr_hbm, sums_ref, vec_ref = refs[15:19]
    R = Refs()
    for name, r in zip(list(SCRATCH) + list(comm_scratch(CH, 16, 1)), refs[19:]):
        setattr(R, name, r)
    R.wo_ref, R.wu_ref, R.wd_ref = ws[7], ws[11], ws[13]
    R.bwd1_done = 44
    aln, acc, ones_acc, send_buf, recv_buf, vec_send, vec_recv = R.aln, R.acc, R.ones_acc, R.send_buf, R.recv_buf, R.vec_send, R.vec_recv
    rs_send, rs_recv, ag_send, ag_recv, vs_send, vs_recv = R.rs_send, R.rs_recv, R.ag_send, R.ag_recv, R.vs_send, R.vs_recv
    rows = R.xv.shape[0]
    blocks = rows // CH
    section = lax.axis_index("section")
    dp = lax.axis_index("dp")
    orders = plan(dp_bits)

    def bit_of(axis, weight):
        return section if axis == "section" else lax.rem(lax.div(dp, weight), 2)

    def across(axis, weight):
        v = bit_of(axis, weight)
        if axis == "section":
            return (1 - section, dp)
        return (section, dp + (1 - 2 * v) * weight)

    barrier = pltpu.get_barrier_semaphore()
    for axis, weight in orders[0]:
        pl.semaphore_signal(barrier, inc=1, device_id=across(axis, weight), device_id_type=MESH)

    def fetch(b, k):
        src = (x_hbm, e_hbm, g_hbm)[k]
        dst = (R.xv, R.ev, R.gv)[k]
        start = pl.multiple_of(b * CH, CH)
        return pltpu.make_async_copy(
            src.at[pl.ds(pl.multiple_of(section * rows, CH) + start, CH), :],
            dst.at[pl.ds(start, CH), :], R.in_sem.at[b, k])

    def start_fetches(b, c):
        for k in range(3):
            fetch(b, k).start()
        return c
    lax.fori_loop(0, blocks, start_fetches, 0)

    prologue(R, *ws)
    acc[...] = jnp.zeros_like(acc)
    ones_acc[...] = jnp.zeros_like(ones_acc)
    prompts = rows // SLOTS
    at_most = lengths_ref.shape[1]
    j_iota = lax.broadcasted_iota(jnp.int32, (1, at_most), 1)
    for p in range(prompts):
        count = counts_ref[section * prompts + p]
        kept = jnp.where(j_iota < count, lengths_ref[pl.ds(section * prompts + p, 1), :], 0)
        total = jnp.sum(kept.astype(F32), axis=1, keepdims=True).astype(jnp.int32)
        R.used_v[p:p + 1, :] = jnp.broadcast_to(total, (1, 128))

    k_iota = lax.broadcasted_iota(jnp.int32, (KEYS, SLOTS), 0)
    q_iota = lax.broadcasted_iota(jnp.int32, (KEYS, SLOTS), 1)

    def out_copies(b, k):
        stage, out = ((R.stS, st_hbm), (R.grS, gr_hbm))[k]
        here = pl.ds(pl.multiple_of(b * CH, CH), CH)
        there = pl.ds(pl.multiple_of(section * rows, CH) + pl.multiple_of(b * CH, CH), CH)
        own = pltpu.make_async_copy(stage.at[section, here, :], out.at[there, :], R.local_sem.at[b, k])
        sent = pltpu.make_async_remote_copy(
            src_ref=stage.at[1 - section, here, :], dst_ref=out.at[there, :],
            send_sem=R.ex_send.at[b, k], recv_sem=R.ex_recv.at[b, k],
            device_id=(1 - section, dp), device_id_type=MESH)
        return own, sent

    def add_wd(i, t):
        n = min(256, FF - i)
        acc[i:i + n, :] += t[0:n]
        if t.shape[0] > n:
            ones_acc[0] += t[n:]

    def add_wu(j, t):
        acc[FF + j * D:FF + j * D + D, :] += t[0:D]
        ones_acc[1 + j] += t[D:]

    def add_wqkv(j, t):
        acc[2 * FF + j * D:2 * FF + j * D + D, :] += t[0:D]
        ones_acc[5 + j] += t[D:]

    def add_wo(t):
        acc[2 * FF + 3 * D:2 * FF + 4 * D, :] += t[0:D]
        ones_acc[8] += t[D:]
    R.add_wd, R.add_wu, R.add_wqkv, R.add_wo = add_wd, add_wu, add_wqkv, add_wo

    pl.semaphore_wait(barrier, len(orders[0]))

    def group(g, carry):
        def at(b):
            return pl.ds(pl.multiple_of(g * GROUP + b, 128), 128)

        def load(c):
            b = g * (GROUP // CH) + c
            for k in range(3):
                fetch(b, k).wait()
            tok = slice(c * CH, c * CH + CH)
            src = pl.ds(pl.multiple_of(b * CH, CH), CH)
            e = R.ev[src, :].T
            R.eT[:, tok] = e
            R.uT[:, tok] = R.xv[src, :].T.astype(F32) + e.astype(F32)
            grad = R.gv[src, :].T
            R.gT[:, tok] = grad.astype(F32)
            R.lowT[1, :, tok] = grad
        R.load = load

        def finish_forward(it, b, out):
            R.stS[it, at(b), :] = out.T
            if it == 0:
                R.uT[:, b:b + 128] = out.astype(F32) + R.eT[:, b:b + 128].astype(F32)
        R.finish_forward = finish_forward

        def finish_backward(it, b, low):
            R.grS[it, at(b), :] = low.T
            if it == 1:
                R.gT[:, b:b + 128] = low.astype(F32)
                R.lowT[0, :, b:b + 128] = low
        R.finish_backward = finish_backward

        def send(c, k):
            for copy in out_copies(g * (GROUP // CH) + c, k):
                copy.start()
        R.send = send

        masks = []
        for p in range(PG):
            used = R.used_v[pl.ds(g * PG + p, 1), :]
            masks.append(jnp.where((k_iota <= q_iota) & (k_iota < used), 0.0, -1e30).astype(F32))
        run_group(R, masks, LAG)
        return carry

    lax.fori_loop(0, rows // GROUP, group, 0)

    for i, j in enumerate((0, 1, 5, 6)):
        vec_ref[j:j + 1, :] = jnp.sum(aln[i].T, axis=0, keepdims=True)
    for i, j in ((0, 7), (1, 8), (2, 9), (3, 10), (4, 11), (5, 2), (7, 3), (8, 4)):
        vec_ref[j:j + 1, :] = ones_acc[i, 0:1, :]
    vec_ref[12:16, :] = jnp.zeros((4, D), F32)

    total_rows = acc.shape[0]
    part_rows = total_rows // PARTS
    offs = [p * part_rows for p in range(PARTS)]
    sizes = [part_rows] * PARTS
    pending = [None] * PARTS
    history = [[] for _ in range(PARTS)]
    used_rows = 0
    vec_pending = None

    def finish_vec():
        nonlocal vec_pending
        if vec_pending is not None:
            copy, s = vec_pending
            copy.wait()
            vec_ref[...] = vec_ref[...] + vec_recv[s]
            vec_pending = None

    for s in range(len(orders[0])):
        for p in range(PARTS):
            if pending[p] is not None:
                pending[p]()
            axis, weight = orders[p][s]
            v = bit_of(axis, weight)
            off, size = offs[p], sizes[p]
            halve = size >= 32
            n = size // 2 if halve else size
            src_off = pl.multiple_of(off + (1 - v) * n, 16) if halve else off
            keep = pl.multiple_of(off + v * n, 16) if halve else off
            region = pl.ds(used_rows, n)
            used_rows += n
            send_buf[region, :] = acc[pl.ds(src_off, n), :].astype(BF)
            copy = pltpu.make_async_remote_copy(
                src_ref=send_buf.at[region, :], dst_ref=recv_buf.at[region, :],
                send_sem=rs_send.at[s, p], recv_sem=rs_recv.at[s, p],
                device_id=across(axis, weight), device_id_type=MESH)
            copy.start()

            def finish(copy=copy, keep=keep, n=n, region=region, halve=halve):
                copy.wait()
                own = acc[pl.ds(keep, n), :]
                if not halve:
                    own = own.astype(BF).astype(F32)
                acc[pl.ds(keep, n), :] = own + recv_buf[region, :].astype(F32)
            pending[p] = finish
            if halve:
                history[p].append((axis, weight, off, n, keep))
                offs[p], sizes[p] = keep, n
        finish_vec()
        axis, weight = orders[0][s]
        vec_send[s] = vec_ref[...]
        copy = pltpu.make_async_remote_copy(
            src_ref=vec_send.at[s], dst_ref=vec_recv.at[s],
            send_sem=vs_send.at[s], recv_sem=vs_recv.at[s],
            device_id=across(axis, weight), device_id_type=MESH)
        copy.start()
        vec_pending = (copy, s)
    finish_vec()
    for p in range(PARTS):
        pending[p]()
        sums_ref[pl.ds(offs[p], sizes[p]), :] = acc[pl.ds(offs[p], sizes[p]), :].astype(BF)
    last = [None] * PARTS
    for s in range(max(len(h) for h in history)):
        for p in range(PARTS):
            if last[p] is not None:
                last[p].wait()
            axis, weight, off, n, keep = history[p][-1 - s]
            copy = pltpu.make_async_remote_copy(
                src_ref=sums_ref.at[pl.ds(keep, n), :], dst_ref=sums_ref.at[pl.ds(keep, n), :],
                send_sem=ag_send.at[s, p], recv_sem=ag_recv.at[s, p],
                device_id=across(axis, weight), device_id_type=MESH)
            copy.start()
            last[p] = copy
    for p in range(PARTS):
        last[p].wait()

    def finish_out(b, c):
        for k in range(2):
            own, sent = out_copies(b, k)
            own.wait()
            sent.wait()
        return c
    lax.fori_loop(0, blocks, finish_out, 0)


def compute(x, e, g, counts, lengths, params, dp_size):
    local = x.shape[0]
    rows = local // 2
    dp_bits = dp_size.bit_length() - 1
    stages = dp_bits + 1
    hbm = pl.BlockSpec(memory_space=pl.ANY)
    smem = pl.BlockSpec(memory_space=pltpu.SMEM)
    vmem = pl.BlockSpec(memory_space=pltpu.VMEM)
    outs = [
        jax.ShapeDtypeStruct((local, 256), BF),
        jax.ShapeDtypeStruct((local, 256), BF),
        jax.ShapeDtypeStruct((3072, 256), BF),
        jax.ShapeDtypeStruct((16, 256), F32),
    ]
    buf_rows = 0
    size = 3072 // PARTS
    for _ in range(stages):
        n = size // 2 if size >= 32 else size
        buf_rows += n * PARTS
        size = n
    return pl.pallas_call(
        functools.partial(kernel, dp_bits),
        out_shape=outs,
        in_specs=[hbm, hbm, hbm, smem, vmem] + [vmem] * 15,
        out_specs=[hbm, hbm, vmem, vmem],
        scratch_shapes=[pltpu.VMEM(s, t) for s, t in SCRATCH.values()] + list(comm_scratch(rows, buf_rows, stages).values()),
        compiler_params=pltpu.CompilerParams(
            vmem_limit_bytes=62 * 1024 * 1024, collective_id=0, has_side_effects=True),
    )(x, e, g, counts, lengths, *params)


def widen_kernel(st_ref, gr_ref, sums_ref, vec_ref, st_out, gr_out, n1g, n1b, wq, qb, wk, wv, vb, wo, ob, n2g, n2b, wu, ub, wd, db):
    st_out[0] = st_ref[...]
    gr_out[0] = gr_ref[...].astype(F32)

    @pl.when(pl.program_id(0) == 0)
    def _():
        wd[...] = sums_ref[0:1024, :].astype(F32)
        for j in range(4):
            wu[:, 256 * j:256 * j + 256] = sums_ref[1024 + 256 * j:1280 + 256 * j, :].astype(F32)
            ub[256 * j:256 * j + 256] = vec_ref[8 + j]
        for j, r in enumerate((wq, wk, wv, wo)):
            r[...] = sums_ref[2048 + 256 * j:2304 + 256 * j, :].astype(F32)
        for j, r in enumerate((n1g, n1b, qb, vb, ob, n2g, n2b, db)):
            r[...] = vec_ref[j]


def widen(st, gr, sums, vec, params):
    local = st.shape[0]
    block = min(512, local)
    full = lambda a: pl.BlockSpec(a.shape, lambda i: (0,) * a.ndim)
    outs = [jax.ShapeDtypeStruct((1, local, 256), BF), jax.ShapeDtypeStruct((1, local, 256), F32)]
    outs += [jax.ShapeDtypeStruct(p.shape, F32) for p in params]
    blk = pl.BlockSpec((block, 256), lambda i: (i, 0))
    oblk = pl.BlockSpec((1, block, 256), lambda i: (0, i, 0))
    return pl.pallas_call(
        widen_kernel,
        grid=(local // block,),
        out_shape=outs,
        in_specs=[blk, blk, full(sums), full(vec)],
        out_specs=[oblk, oblk] + [full(o) for o in outs[2:]],
        compiler_params=pltpu.CompilerParams(vmem_limit_bytes=60 * 1024 * 1024),
    )(st, gr, sums, vec)


def solution(mesh):
    dp_size = mesh.shape["dp"]

    def body(x, e, g, counts, lengths, *params):
        st, gr, sums, vec = compute(x, e, g, counts, lengths, params, dp_size)
        return tuple(widen(st, gr, sums, vec, params))

    placed = (P("dp", None),) * 3 + (P("dp"), P("dp", None)) + (P(),) * 15
    return jax.shard_map(
        body,
        mesh=mesh,
        in_specs=placed,
        out_specs=(P("section", "dp", None),) * 2 + (P(),) * 15,
        check_vma=False,
    )
```

time: 154 us -> 114 us (0.74)
  Pallas kernels: 147 us -> 113 us
  local copies, waits for them, and re-layouts: 5.3 us -> 0 us
    pallas_call x1, Pallas kernels: 142 us -> 105 us  [compute(): pl.pallas_call(functools.partial(kernel, dp_bits), out_shape=outs, in_spe...]
    unnamed x8 -> x0, local copies, waits for them, and re-layouts: 5.3 us -> none
    pallas_call x1, Pallas kernels: 5.2 us -> 8.8 us  [widen(): pl.pallas_call(widen_kernel, grid=(local // block,), out_shape=outs, in_s...]
where the time goes in v3:
time: 114 us
  Pallas kernels  113 us (99%)
    pallas_call x1, Pallas kernels, compute(): pl.pallas_call(functools.partial(kernel, dp_bits), out_shape=outs, in_spe...  105 us
    pallas_call x1, Pallas kernels, widen(): pl.pallas_call(widen_kernel, grid=(local // block,), out_shape=outs, in_s...  8.8 us

profile of v3, /device:TPU:0, one launch (start us, length us, event | category | flops | bytes accessed | tf_op | source)
XLA Modules:
  0.0 114.1 jit_solution(14324471167470496213)
XLA Ops:
  0.7 104.7 %shard_map.323 = (bf16[4096,256]{1,0:T(8,128)(2,1)}, bf16[4096,256]{1,0:T(8,128)(2,1)}, bf16[3072,256]{1,0:T(8,128)(2,1)}, f32[16,256]{1,0:T(8,128)}) custom-call(bf16[4096,256]{1,0:T(8,128)(2,1)} %x_hbm.1, bf16[4096,256]{1,0:T(8,128)(2,1)} %e_hbm.1, bf16[4096,256]{1,0:T(8,128)(2,1)} %g_hbm.1, s32[32]{0:T(128)} %counts_ref.1, s32[32,50]{1,0:T(8,128)} %lengths_ref.1, ...), custom_call_target="tpu_custom_call" | custom-call | tf_op jit(solution)/shard_map/pallas_call | solution.py:556
  105.3 8.8 %shard_map.324 = (bf16[1,4096,256]{2,1,0:T(8,128)(2,1)}, f32[1,4096,256]{2,1,0:T(8,128)}, f32[256]{0:T(256)}, f32[256]{0:T(256)}, f32[256,256]{1,0:T(8,128)}, /*...) custom-call(bf16[4096,256]{1,0:T(8,128)(2,1)} %get-tuple-element.21., ...), custom_call_target="tpu_custom_call" | custom-call | tf_op jit(solution)/shard_map/pallas_call | solution.py:591

commit v4 on v3

--- a/solution.py
+++ b/solution.py
@@ -283,59 +283,183 @@
 
 LAG = 3
 MESH = pl.DeviceIdType.MESH
-PARTS = 3
-
-
-def plan(dp_bits):
-    first = [("dp", 1)]
-    turned = [("dp", 2), ("section", 1), ("dp", 4)]
-    last = [("dp", 1 << b) for b in range(3, dp_bits)]
-    return [first + turned[p:] + turned[:p] + last for p in range(PARTS)]
-
-
-def comm_scratch(rows, buf_rows, stages):
+CUBE = (("dp", 2), ("section", 1), ("dp", 4))
+PEERS = 7
+
+
+class Place:
+    def __init__(self, dp_bits):
+        self.section = lax.axis_index("section")
+        self.dp = lax.axis_index("dp")
+        self.core = lax.rem(self.dp, 2)
+        self.rest = [1 << b for b in range(3, dp_bits)]
+        self.bits = [self.bit(axis, weight) for axis, weight in CUBE]
+        self.cube = self.bits[0] + 2 * self.bits[1] + 4 * self.bits[2]
+
+    def bit(self, axis, weight):
+        return self.section if axis == "section" else lax.rem(lax.div(self.dp, weight), 2)
+
+    def across(self, axis, weight):
+        if axis == "section":
+            return (1 - self.section, self.dp)
+        return (self.section, self.dp + (1 - 2 * self.bit(axis, weight)) * weight)
+
+    def peer(self, mask):
+        section, dp, number = self.section, self.dp, 0
+        for i, (axis, weight) in enumerate(CUBE):
+            v = self.bits[i]
+            if mask >> i & 1:
+                if axis == "section":
+                    section = 1 - section
+                else:
+                    dp = dp + (1 - 2 * v) * weight
+                v = 1 - v
+            number = number + v * (1 << i)
+        return (section, dp), number
+
+    def everyone(self):
+        found = [self.across("dp", 1)] + [self.peer(m)[0] for m in range(1, PEERS + 1)]
+        return found + [self.across("dp", w) for w in self.rest]
+
+
+class Sums:
+    def __init__(self, R, place, e, base, rows):
+        self.R, self.place, self.e, self.base = R, place, e, base
+        self.half, self.n = rows // 2, rows // 16
+        self.sent = []
+        self.buf = base // 2
+        self.cbuf = base // 16
+        self.keep = pl.multiple_of(base + place.core * self.half, 16)
+        self.own = pl.multiple_of(self.keep + place.cube * self.n, 16)
+
+    def copy(self, src, dst, slot, device):
+        R = self.R
+        c = pltpu.make_async_remote_copy(src_ref=src, dst_ref=dst, send_sem=R.sum_send.at[self.e, slot],
+                                         recv_sem=R.sum_recv.at[self.e, slot], device_id=device, device_id_type=MESH)
+        c.start()
+        self.sent.append(c)
+        return c
+
+    def steps(self):
+        R, place, half, n = self.R, self.place, self.half, self.n
+        region = pl.ds(self.buf, half)
+        away = pl.multiple_of(self.base + (1 - place.core) * half, 16)
+        R.core_send[region, :] = R.acc[pl.ds(away, half), :].astype(BF)
+        c = self.copy(R.core_send.at[region, :], R.core_recv.at[region, :], 0, place.across("dp", 1))
+        yield
+        c.wait_recv()
+        small = pl.ds(self.cbuf, n)
+        waits = []
+        for m in range(1, PEERS + 1):
+            device, number = place.peer(m)
+            at = pl.multiple_of(number * n, 16)
+            R.cube_send[m - 1, small, :] = (R.acc[pl.ds(pl.multiple_of(self.keep + at, 16), n), :]
+                                            + R.core_recv[pl.ds(pl.multiple_of(self.buf + at, 16), n), :].astype(F32)).astype(BF)
+            waits.append(self.copy(R.cube_send.at[m - 1, small, :], R.cube_recv.at[m - 1, small, :], m, device))
+        total = R.acc[pl.ds(self.own, n), :] + R.core_recv[pl.ds(pl.multiple_of(self.buf + place.cube * n, 16), n), :].astype(F32)
+        R.acc[pl.ds(self.own, n), :] = total
+        yield
+        for c in waits:
+            c.wait_recv()
+        total = R.acc[pl.ds(self.own, n), :]
+        for m in range(PEERS):
+            total = total + R.cube_recv[m, small, :].astype(F32)
+        for i, weight in enumerate(place.rest):
+            R.rest_send[i, small, :] = total.astype(BF)
+            c = self.copy(R.rest_send.at[i, small, :], R.rest_recv.at[i, small, :], 2 * PEERS + 2 + i, place.across("dp", weight))
+            yield
+            c.wait_recv()
+            total = R.rest_send[i, small, :].astype(F32) + R.rest_recv[i, small, :].astype(F32)
+        own = pl.ds(self.own, n)
+        R.sums[own, :] = total.astype(BF)
+        waits = []
+        for m in range(1, PEERS + 1):
+            waits.append(self.copy(R.sums.at[own, :], R.sums.at[own, :], PEERS + m, place.peer(m)[0]))
+        yield
+        for c in waits:
+            c.wait_recv()
+        keep = pl.ds(self.keep, half)
+        c = self.copy(R.sums.at[keep, :], R.sums.at[keep, :], 2 * PEERS + 1, place.across("dp", 1))
+        yield
+        c.wait_recv()
+
+    def finish(self):
+        for c in self.sent:
+            c.wait_send()
+
+
+class VectorSums(Sums):
+    def __init__(self, R, place, e):
+        self.R, self.place, self.e = R, place, e
+        self.sent = []
+
+    def steps(self):
+        R, place = self.R, self.place
+        R.vec_send[0] = R.vec[...]
+        c = self.copy(R.vec_send.at[0], R.vec_recv.at[0], 0, place.across("dp", 1))
+        yield
+        c.wait_recv()
+        R.vec_cube[place.cube] = R.vec_send[0] + R.vec_recv[0]
+        waits = []
+        for m in range(1, PEERS + 1):
+            waits.append(self.copy(R.vec_cube.at[place.cube], R.vec_cube.at[place.cube], m, place.peer(m)[0]))
+        yield
+        for c in waits:
+            c.wait_recv()
+        total = R.vec_cube[0]
+        for i in range(1, PEERS + 1):
+            total = total + R.vec_cube[i]
+        for i, weight in enumerate(place.rest):
+            R.vec_send[1 + i] = total
+            c = self.copy(R.vec_send.at[1 + i], R.vec_recv.at[1 + i], 2 * PEERS + 2 + i, place.across("dp", weight))
+            yield
+            c.wait_recv()
+            total = R.vec_send[1 + i] + R.vec_recv[1 + i]
+        R.vec[...] = total
+
+
+FF_ROWS = 2 * FF + D
+QKV_ROWS = 3 * D
+
+
+def comm_scratch(rows, rest):
     blocks = rows // CH
     dma = pltpu.SemaphoreType.DMA
+    total = FF_ROWS + QKV_ROWS
+    slots = 2 * PEERS + 2 + rest
     return dict(
         xv=pltpu.VMEM((rows, 256), BF), ev=pltpu.VMEM((rows, 256), BF), gv=pltpu.VMEM((rows, 256), BF),
         stS=pltpu.VMEM((2, rows, 256), BF), grS=pltpu.VMEM((2, rows, 256), BF),
         used_v=pltpu.VMEM((rows // SLOTS, 128), jnp.int32),
-        acc=pltpu.VMEM((3072, 256), F32), ones_acc=pltpu.VMEM((9, 16, 256), F32),
-        send_buf=pltpu.VMEM((buf_rows, 256), BF), recv_buf=pltpu.VMEM((buf_rows, 256), BF),
-        vec_send=pltpu.VMEM((stages, 16, 256), F32), vec_recv=pltpu.VMEM((stages, 16, 256), F32),
+        acc=pltpu.VMEM((total, 256), F32), ones_acc=pltpu.VMEM((9, 16, 256), F32),
+        core_send=pltpu.VMEM((total // 2, 256), BF), core_recv=pltpu.VMEM((total // 2, 256), BF),
+        cube_send=pltpu.VMEM((PEERS, total // 16, 256), BF), cube_recv=pltpu.VMEM((PEERS, total // 16, 256), BF),
+        rest_send=pltpu.VMEM((rest, total // 16, 256), BF), rest_recv=pltpu.VMEM((rest, total // 16, 256), BF),
+        vec_send=pltpu.VMEM((1 + rest, 16, 256), F32), vec_recv=pltpu.VMEM((1 + rest, 16, 256), F32),
+        vec_cube=pltpu.VMEM((PEERS + 1, 16, 256), F32),
         in_sem=dma((blocks, 3)), local_sem=dma((blocks, 2)), ex_send=dma((blocks, 2)), ex_recv=dma((blocks, 2)),
-        rs_send=dma((stages, PARTS)), rs_recv=dma((stages, PARTS)), ag_send=dma((stages, PARTS)), ag_recv=dma((stages, PARTS)),
-        vs_send=dma((stages,)), vs_recv=dma((stages,)))
+        sum_send=dma((3, slots)), sum_recv=dma((3, slots)))
 
 
 def kernel(dp_bits, x_hbm, e_hbm, g_hbm, counts_ref, lengths_ref, *refs):
     ws = refs[:15]
     st_hbm, gr_hbm, sums_ref, vec_ref = refs[15:19]
     R = Refs()
-    for name, r in zip(list(SCRATCH) + list(comm_scratch(CH, 16, 1)), refs[19:]):
+    for name, r in zip(list(SCRATCH) + list(comm_scratch(CH, 1)), refs[19:]):
         setattr(R, name, r)
     R.wo_ref, R.wu_ref, R.wd_ref = ws[7], ws[11], ws[13]
+    R.sums, R.vec = sums_ref, vec_ref
     R.bwd1_done = 44
-    aln, acc, ones_acc, send_buf, recv_buf, vec_send, vec_recv = R.aln, R.acc, R.ones_acc, R.send_buf, R.recv_buf, R.vec_send, R.vec_recv
-    rs_send, rs_recv, ag_send, ag_recv, vs_send, vs_recv = R.rs_send, R.rs_recv, R.ag_send, R.ag_recv, R.vs_send, R.vs_recv
+    aln, acc, ones_acc = R.aln, R.acc, R.ones_acc
     rows = R.xv.shape[0]
     blocks = rows // CH
-    section = lax.axis_index("section")
-    dp = lax.axis_index("dp")
-    orders = plan(dp_bits)
-
-    def bit_of(axis, weight):
-        return section if axis == "section" else lax.rem(lax.div(dp, weight), 2)
-
-    def across(axis, weight):
-        v = bit_of(axis, weight)
-        if axis == "section":
-            return (1 - section, dp)
-        return (section, dp + (1 - 2 * v) * weight)
+    place = Place(dp_bits)
+    section, dp = place.section, place.dp
 
     barrier = pltpu.get_barrier_semaphore()
-    for axis, weight in orders[0]:
-        pl.semaphore_signal(barrier, inc=1, device_id=across(axis, weight), device_id_type=MESH)
+    everyone = place.everyone()
+    for device in everyone:
+        pl.semaphore_signal(barrier, inc=1, device_id=device, device_id_type=MESH)
 
     def fetch(b, k):
         src = (x_hbm, e_hbm, g_hbm)[k]
@@ -388,15 +512,15 @@
         ones_acc[1 + j] += t[D:]
 
     def add_wqkv(j, t):
-        acc[2 * FF + j * D:2 * FF + j * D + D, :] += t[0:D]
+        acc[FF_ROWS + j * D:FF_ROWS + j * D + D, :] += t[0:D]
         ones_acc[5 + j] += t[D:]
 
     def add_wo(t):
-        acc[2 * FF + 3 * D:2 * FF + 4 * D, :] += t[0:D]
+        acc[2 * FF:2 * FF + D, :] += t[0:D]
         ones_acc[8] += t[D:]
     R.add_wd, R.add_wu, R.add_wqkv, R.add_wo = add_wd, add_wu, add_wqkv, add_wo
 
-    pl.semaphore_wait(barrier, len(orders[0]))
+    pl.semaphore_wait(barrier, len(everyone))
 
     def group(g, carry):
         def at(b):
@@ -449,80 +573,16 @@
         vec_ref[j:j + 1, :] = ones_acc[i, 0:1, :]
     vec_ref[12:16, :] = jnp.zeros((4, D), F32)
 
-    total_rows = acc.shape[0]
-    part_rows = total_rows // PARTS
-    offs = [p * part_rows for p in range(PARTS)]
-    sizes = [part_rows] * PARTS
-    pending = [None] * PARTS
-    history = [[] for _ in range(PARTS)]
-    used_rows = 0
-    vec_pending = None
-
-    def finish_vec():
-        nonlocal vec_pending
-        if vec_pending is not None:
-            copy, s = vec_pending
-            copy.wait()
-            vec_ref[...] = vec_ref[...] + vec_recv[s]
-            vec_pending = None
-
-    for s in range(len(orders[0])):
-        for p in range(PARTS):
-            if pending[p] is not None:
-                pending[p]()
-            axis, weight = orders[p][s]
-            v = bit_of(axis, weight)
-            off, size = offs[p], sizes[p]
-            halve = size >= 32
-            n = size // 2 if halve else size
-            src_off = pl.multiple_of(off + (1 - v) * n, 16) if halve else off
-            keep = pl.multiple_of(off + v * n, 16) if halve else off
-            region = pl.ds(used_rows, n)
-            used_rows += n
-            send_buf[region, :] = acc[pl.ds(src_off, n), :].astype(BF)
-            copy = pltpu.make_async_remote_copy(
-                src_ref=send_buf.at[region, :], dst_ref=recv_buf.at[region, :],
-                send_sem=rs_send.at[s, p], recv_sem=rs_recv.at[s, p],
-                device_id=across(axis, weight), device_id_type=MESH)
-            copy.start()
-
-            def finish(copy=copy, keep=keep, n=n, region=region, halve=halve):
-                copy.wait()
-                own = acc[pl.ds(keep, n), :]
-                if not halve:
-                    own = own.astype(BF).astype(F32)
-                acc[pl.ds(keep, n), :] = own + recv_buf[region, :].astype(F32)
-            pending[p] = finish
-            if halve:
-                history[p].append((axis, weight, off, n, keep))
-                offs[p], sizes[p] = keep, n
-        finish_vec()
-        axis, weight = orders[0][s]
-        vec_send[s] = vec_ref[...]
-        copy = pltpu.make_async_remote_copy(
-            src_ref=vec_send.at[s], dst_ref=vec_recv.at[s],
-            send_sem=vs_send.at[s], recv_sem=vs_recv.at[s],
-            device_id=across(axis, weight), device_id_type=MESH)
-        copy.start()
-        vec_pending = (copy, s)
-    finish_vec()
-    for p in range(PARTS):
-        pending[p]()
-        sums_ref[pl.ds(offs[p], sizes[p]), :] = acc[pl.ds(offs[p], sizes[p]), :].astype(BF)
-    last = [None] * PARTS
-    for s in range(max(len(h) for h in history)):
-        for p in range(PARTS):
-            if last[p] is not None:
-                last[p].wait()
-            axis, weight, off, n, keep = history[p][-1 - s]
-            copy = pltpu.make_async_remote_copy(
-                src_ref=sums_ref.at[pl.ds(keep, n), :], dst_ref=sums_ref.at[pl.ds(keep, n), :],
-                send_sem=ag_send.at[s, p], recv_sem=ag_recv.at[s, p],
-                device_id=across(axis, weight), device_id_type=MESH)
-            copy.start()
-            last[p] = copy
-    for p in range(PARTS):
-        last[p].wait()
+    sums = [Sums(R, place, 0, 0, FF_ROWS), Sums(R, place, 1, FF_ROWS, QKV_ROWS), VectorSums(R, place, 2)]
+    running = [x.steps() for x in sums]
+    while running:
+        for x in list(running):
+            try:
+                next(x)
+            except StopIteration:
+                running.remove(x)
+    for x in sums:
+        x.finish()
 
     def finish_out(b, c):
         for k in range(2):
@@ -537,7 +597,7 @@
     local = x.shape[0]
     rows = local // 2
     dp_bits = dp_size.bit_length() - 1
-    stages = dp_bits + 1
+    rest = dp_bits - 3
     hbm = pl.BlockSpec(memory_space=pl.ANY)
     smem = pl.BlockSpec(memory_space=pltpu.SMEM)
     vmem = pl.BlockSpec(memory_space=pltpu.VMEM)
@@ -547,53 +607,84 @@
         jax.ShapeDtypeStruct((3072, 256), BF),
         jax.ShapeDtypeStruct((16, 256), F32),
     ]
-    buf_rows = 0
-    size = 3072 // PARTS
-    for _ in range(stages):
-        n = size // 2 if size >= 32 else size
-        buf_rows += n * PARTS
-        size = n
     return pl.pallas_call(
         functools.partial(kernel, dp_bits),
         out_shape=outs,
         in_specs=[hbm, hbm, hbm, smem, vmem] + [vmem] * 15,
         out_specs=[hbm, hbm, vmem, vmem],
-        scratch_shapes=[pltpu.VMEM(s, t) for s, t in SCRATCH.values()] + list(comm_scratch(rows, buf_rows, stages).values()),
+        scratch_shapes=[pltpu.VMEM(s, t) for s, t in SCRATCH.values()] + list(comm_scratch(rows, rest).values()),
         compiler_params=pltpu.CompilerParams(
             vmem_limit_bytes=62 * 1024 * 1024, collective_id=0, has_side_effects=True),
     )(x, e, g, counts, lengths, *params)
 
 
-def widen_kernel(st_ref, gr_ref, sums_ref, vec_ref, st_out, gr_out, n1g, n1b, wq, qb, wk, wv, vb, wo, ob, n2g, n2b, wu, ub, wd, db):
-    st_out[0] = st_ref[...]
-    gr_out[0] = gr_ref[...].astype(F32)
-
-    @pl.when(pl.program_id(0) == 0)
-    def _():
-        wd[...] = sums_ref[0:1024, :].astype(F32)
-        for j in range(4):
-            wu[:, 256 * j:256 * j + 256] = sums_ref[1024 + 256 * j:1280 + 256 * j, :].astype(F32)
-            ub[256 * j:256 * j + 256] = vec_ref[8 + j]
-        for j, r in enumerate((wq, wk, wv, wo)):
-            r[...] = sums_ref[2048 + 256 * j:2304 + 256 * j, :].astype(F32)
-        for j, r in enumerate((n1g, n1b, qb, vb, ob, n2g, n2b, db)):
-            r[...] = vec_ref[j]
+CHUNKS = 8
+
+
+def widen_kernel(st_ref, gr_ref, sums_ref, vec_ref, st_out, gr_out, n1g, n1b, wq, qb, wk, wv, vb, wo, ob, n2g, n2b, wu, ub, wd, db,
+                 st_v, gr_v, gr_w, sums_v, wd_v, wu_v, wa_v, st_in, gr_in, sum_in, st_sem, gr_sem, w_sem):
+    block = st_v.shape[0] // CHUNKS
+    sums_in = [pltpu.make_async_copy(sums_ref.at[rows, :], sums_v.at[rows, :], sum_in.at[i])
+               for i, rows in enumerate((pl.ds(0, FF), pl.ds(FF, FF + D + QKV_ROWS)))]
+    parts = [pl.ds(i * block, block) for i in range(CHUNKS)]
+    gr_ins = [pltpu.make_async_copy(gr_ref.at[r, :], gr_v.at[r, :], gr_in.at[i]) for i, r in enumerate(parts)]
+    st_ins = [pltpu.make_async_copy(st_ref.at[r, :], st_v.at[r, :], st_in.at[i]) for i, r in enumerate(parts)]
+    outs = []
+
+    def out(src, dst, sem):
+        c = pltpu.make_async_copy(src, dst, sem)
+        c.start()
+        outs.append(c)
+
+    for c in gr_ins[:2] + sums_in + gr_ins[2:] + st_ins:
+        c.start()
+
+    def gradients(i):
+        gr_ins[i].wait()
+        gr_w[parts[i], :] = gr_v[parts[i], :].astype(F32)
+        out(gr_w.at[parts[i], :], gr_out.at[0, parts[i], :], gr_sem.at[i])
+
+    gradients(0)
+    gradients(1)
+    sums_in[0].wait()
+    wd_v[...] = sums_v[0:FF, :].astype(F32)
+    out(wd_v, wd, w_sem.at[0])
+    sums_in[1].wait()
+    for j in range(FF // D):
+        wu_v[:, D * j:D * j + D] = sums_v[FF + D * j:FF + D * j + D, :].astype(F32)
+    out(wu_v, wu, w_sem.at[1])
+    wa_v[...] = sums_v[2 * FF:2 * FF + 4 * D, :].astype(F32)
+    for j, r in enumerate((wo, wq, wk, wv)):
+        out(wa_v.at[D * j:D * j + D, :], r, w_sem.at[2 + j])
+    for i in range(2, CHUNKS):
+        gradients(i)
+    for j in range(FF // D):
+        ub[D * j:D * j + D] = vec_ref[8 + j]
+    for j, r in enumerate((n1g, n1b, qb, vb, ob, n2g, n2b, db)):
+        r[...] = vec_ref[j]
+    for i in range(CHUNKS):
+        st_ins[i].wait()
+        out(st_v.at[parts[i], :], st_out.at[0, parts[i], :], st_sem.at[i])
+    for c in outs:
+        c.wait()
 
 
 def widen(st, gr, sums, vec, params):
     local = st.shape[0]
-    block = min(512, local)
-    full = lambda a: pl.BlockSpec(a.shape, lambda i: (0,) * a.ndim)
     outs = [jax.ShapeDtypeStruct((1, local, 256), BF), jax.ShapeDtypeStruct((1, local, 256), F32)]
     outs += [jax.ShapeDtypeStruct(p.shape, F32) for p in params]
-    blk = pl.BlockSpec((block, 256), lambda i: (i, 0))
-    oblk = pl.BlockSpec((1, block, 256), lambda i: (0, i, 0))
+    hbm = pl.BlockSpec(memory_space=pl.ANY)
+    vmem = pl.BlockSpec(memory_space=pltpu.VMEM)
+    dma = pltpu.SemaphoreType.DMA
     return pl.pallas_call(
         widen_kernel,
-        grid=(local // block,),
         out_shape=outs,
-        in_specs=[blk, blk, full(sums), full(vec)],
-        out_specs=[oblk, oblk] + [full(o) for o in outs[2:]],
+        in_specs=[hbm, hbm, hbm, vmem],
+        out_specs=[hbm, hbm] + [hbm if len(p.shape) == 2 else vmem for p in params],
+        scratch_shapes=[
+            pltpu.VMEM((local, 256), BF), pltpu.VMEM((local, 256), BF), pltpu.VMEM((local, 256), F32),
+            pltpu.VMEM(sums.shape, BF), pltpu.VMEM((FF, D), F32), pltpu.VMEM((D, FF), F32), pltpu.VMEM((4 * D, D), F32),
+            dma((CHUNKS,)), dma((CHUNKS,)), dma((2,)), dma((CHUNKS,)), dma((CHUNKS,)), dma((6,))],
         compiler_params=pltpu.CompilerParams(vmem_limit_bytes=60 * 1024 * 1024),
     )(st, gr, sums, vec)
 

time: 114 us -> 110 us (0.965)
  Pallas kernels: 113 us -> 109 us
    pallas_call x1, Pallas kernels: 105 us -> 102 us  [compute(): pl.pallas_call(functools.partial(kernel, dp_bits), out_shape=outs, in_spe...]
    pallas_call x1, Pallas kernels: 8.8 us -> 7.54 us  [widen(): pl.pallas_call(widen_kernel, out_shape=outs, in_specs=[hbm, hbm, hbm, vme...]
where the time goes in v4:
time: 110 us
  Pallas kernels  109 us (99%)
    pallas_call x1, Pallas kernels, compute(): pl.pallas_call(functools.partial(kernel, dp_bits), out_shape=outs, in_spe...  102 us
    pallas_call x1, Pallas kernels, widen(): pl.pallas_call(widen_kernel, out_shape=outs, in_specs=[hbm, hbm, hbm, vme...  7.54 us

profile of v4, /device:TPU:0, one launch (start us, length us, event | category | flops | bytes accessed | tf_op | source)
XLA Modules:
  0.0 109.8 jit_solution(1320522473299610088)
XLA Ops:
  0.7 101.6 %shard_map.323 = (bf16[4096,256]{1,0:T(8,128)(2,1)}, bf16[4096,256]{1,0:T(8,128)(2,1)}, bf16[3072,256]{1,0:T(8,128)(2,1)}, f32[16,256]{1,0:T(8,128)}) custom-call(bf16[4096,256]{1,0:T(8,128)(2,1)} %x_hbm.1, bf16[4096,256]{1,0:T(8,128)(2,1)} %e_hbm.1, bf16[4096,256]{1,0:T(8,128)(2,1)} %g_hbm.1, s32[32]{0:T(128)} %counts_ref.1, s32[32,50]{1,0:T(8,128)} %lengths_ref.1, ...), custom_call_target="tpu_custom_call" | custom-call | tf_op jit(solution)/shard_map/pallas_call | solution.py:610
  102.3 7.5 %shard_map.324 = (bf16[1,4096,256]{2,1,0:T(8,128)(2,1)}, f32[1,4096,256]{2,1,0:T(8,128)}, f32[256]{0:T(256)}, f32[256]{0:T(256)}, f32[256,256]{1,0:T(8,128)}, /*...) custom-call(bf16[4096,256]{1,0:T(8,128)(2,1)} %get-tuple-element.21., ...), custom_call_target="tpu_custom_call" | custom-call | tf_op jit(solution)/shard_map/pallas_call | solution.py:679

commit v5 on v4

--- a/solution.py
+++ b/solution.py
@@ -197,8 +197,6 @@
         ln_backward(R.dn, R.gT, R.unit1.at[it], R.inv1.at[it], R.vecs.at[0], R.aln.at[0], R.aln.at[1], R.gT, R.gl16, L)
         for b in range(L.start, L.stop, 128):
             R.finish_backward(it, b, R.gl16[:, b:b + 128])
-        if it == 0:
-            R.send(c, 1)
         yield
 
 
@@ -282,6 +280,7 @@
 
 
 LAG = 3
+LAST_GRADIENTS = 2
 MESH = pl.DeviceIdType.MESH
 CUBE = (("dp", 2), ("section", 1), ("dp", 4))
 PEERS = 7
@@ -438,7 +437,7 @@
         vec_send=pltpu.VMEM((1 + rest, 16, 256), F32), vec_recv=pltpu.VMEM((1 + rest, 16, 256), F32),
         vec_cube=pltpu.VMEM((PEERS + 1, 16, 256), F32),
         in_sem=dma((blocks, 3)), local_sem=dma((blocks, 2)), ex_send=dma((blocks, 2)), ex_recv=dma((blocks, 2)),
-        sum_send=dma((3, slots)), sum_recv=dma((3, slots)))
+        sum_send=dma((4, slots)), sum_recv=dma((4, slots)))
 
 
 def kernel(dp_bits, x_hbm, e_hbm, g_hbm, counts_ref, lengths_ref, *refs):
@@ -563,6 +562,11 @@
             used = R.used_v[pl.ds(g * PG + p, 1), :]
             masks.append(jnp.where((k_iota <= q_iota) & (k_iota < used), 0.0, -1e30).astype(F32))
         run_group(R, masks, LAG)
+
+        @pl.when(g < rows // GROUP - 1)
+        def _():
+            for c in range(GROUP // CH):
+                send(c, 1)
         return carry
 
     lax.fori_loop(0, rows // GROUP, group, 0)
@@ -573,14 +577,20 @@
         vec_ref[j:j + 1, :] = ones_acc[i, 0:1, :]
     vec_ref[12:16, :] = jnp.zeros((4, D), F32)
 
-    sums = [Sums(R, place, 0, 0, FF_ROWS), Sums(R, place, 1, FF_ROWS, QKV_ROWS), VectorSums(R, place, 2)]
+    sums = [Sums(R, place, 0, 0, FF), Sums(R, place, 1, FF, FF_ROWS - FF), Sums(R, place, 2, FF_ROWS, QKV_ROWS), VectorSums(R, place, 3)]
     running = [x.steps() for x in sums]
+    turn = 0
     while running:
         for x in list(running):
             try:
                 next(x)
             except StopIteration:
                 running.remove(x)
+        turn += 1
+        if turn == LAST_GRADIENTS:
+            for c in range(GROUP // CH):
+                for copy in out_copies(blocks - GROUP // CH + c, 1):
+                    copy.start()
     for x in sums:
         x.finish()
 

time: 110 us -> 103 us (0.936)
  Pallas kernels: 109 us -> 103 us
    pallas_call x1, Pallas kernels: 102 us -> 95 us  [compute(): pl.pallas_call(functools.partial(kernel, dp_bits), out_shape=outs, in_spe...]
where the time goes in v5:
time: 103 us
  Pallas kernels  103 us (100%)
    pallas_call x1, Pallas kernels, compute(): pl.pallas_call(functools.partial(kernel, dp_bits), out_shape=outs, in_spe...  95 us
    pallas_call x1, Pallas kernels, widen(): pl.pallas_call(widen_kernel, out_shape=outs, in_specs=[hbm, hbm, hbm, vme...  7.54 us

profile of v5, /device:TPU:0, one launch (start us, length us, event | category | flops | bytes accessed | tf_op | source)
XLA Modules:
  0.0 103.2 jit_solution(5492070379107272347)
XLA Ops:
  0.7 95.0 %shard_map.323 = (bf16[4096,256]{1,0:T(8,128)(2,1)}, bf16[4096,256]{1,0:T(8,128)(2,1)}, bf16[3072,256]{1,0:T(8,128)(2,1)}, f32[16,256]{1,0:T(8,128)}) custom-call(bf16[4096,256]{1,0:T(8,128)(2,1)} %x_hbm.1, bf16[4096,256]{1,0:T(8,128)(2,1)} %e_hbm.1, bf16[4096,256]{1,0:T(8,128)(2,1)} %g_hbm.1, s32[32]{0:T(128)} %counts_ref.1, s32[32,50]{1,0:T(8,128)} %lengths_ref.1, ...), custom_call_target="tpu_custom_call" | custom-call | tf_op jit(solution)/shard_map/pallas_call | solution.py:620
  95.7 7.5 %shard_map.324 = (bf16[1,4096,256]{2,1,0:T(8,128)(2,1)}, f32[1,4096,256]{2,1,0:T(8,128)}, f32[256]{0:T(256)}, f32[256]{0:T(256)}, f32[256,256]{1,0:T(8,128)}, /*...) custom-call(bf16[4096,256]{1,0:T(8,128)(2,1)} %get-tuple-element.21., ...), custom_call_target="tpu_custom_call" | custom-call | tf_op jit(solution)/shard_map/pallas_call | solution.py:689

commit v6 on v5

--- a/solution.py
+++ b/solution.py
@@ -13,6 +13,7 @@
 SLOTS = 128
 HEADS = 8
 KEYS = 112
+USED = 104
 GROUP = 512
 CH = 256
 PG = GROUP // SLOTS
@@ -71,6 +72,7 @@
 def chain(R, c, masks):
     L = slice(c * CH, c * CH + CH)
     prompts = range(c * CH // SLOTS, (c + 1) * CH // SLOTS)
+    rest = jnp.zeros((KEYS - USED, SLOTS), F32)
     R.load(c)
     yield
     for it in range(2):
@@ -98,13 +100,13 @@
             tok = slice(p * 128, p * 128 + 128)
             for h in range(HEADS):
                 ln = slice(128 * h, 128 * h + 128)
-                s = R.sc[p, :, ln] + masks[p]
+                s = R.sc[p, 0:USED, ln] + masks[p]
                 m = jnp.max(s, axis=0, keepdims=True)
                 pe = jnp.exp2((s - m) * (SCALE * math.log2(math.e)))
                 l = jnp.sum(pe, axis=0, keepdims=True)
                 pT = pe * (1.0 / l)
-                R.p32[it, p, :, ln] = pT
-                R.p16[it, p, 0:KEYS, ln] = pT.astype(BF)
+                R.p32[it, p, 0:USED, ln] = pT
+                R.p16[it, p, 0:KEYS, ln] = jnp.concatenate([pT, rest], axis=0).astype(BF)
             yield
             for h2 in range(HEADS // 2):
                 ln = slice(256 * h2, 256 * h2 + 256)
@@ -172,10 +174,10 @@
             tok = slice(p * 128, p * 128 + 128)
             for h in range(HEADS):
                 ln = slice(128 * h, 128 * h + 128)
-                pT = R.p32[it, p, :, ln]
-                t = pT * R.sc[p, :, ln]
+                pT = R.p32[it, p, 0:USED, ln]
+                t = pT * R.sc[p, 0:USED, ln]
                 dsum = jnp.sum(t, axis=0, keepdims=True)
-                R.ds16[p, 0:KEYS, ln] = (t - pT * dsum).astype(BF)
+                R.ds16[p, 0:KEYS, ln] = jnp.concatenate([t - pT * dsum, rest], axis=0).astype(BF)
                 R.dsN[p, :, ln] = R.ds16[p, :, ln].T
             yield
             for h2 in range(HEADS // 2):
@@ -427,7 +429,6 @@
     total = FF_ROWS + QKV_ROWS
     slots = 2 * PEERS + 2 + rest
     return dict(
-        xv=pltpu.VMEM((rows, 256), BF), ev=pltpu.VMEM((rows, 256), BF), gv=pltpu.VMEM((rows, 256), BF),
         stS=pltpu.VMEM((2, rows, 256), BF), grS=pltpu.VMEM((2, rows, 256), BF),
         used_v=pltpu.VMEM((rows // SLOTS, 128), jnp.int32),
         acc=pltpu.VMEM((total, 256), F32), ones_acc=pltpu.VMEM((9, 16, 256), F32),
@@ -450,7 +451,7 @@
     R.sums, R.vec = sums_ref, vec_ref
     R.bwd1_done = 44
     aln, acc, ones_acc = R.aln, R.acc, R.ones_acc
-    rows = R.xv.shape[0]
+    rows = R.stS.shape[1]
     blocks = rows // CH
     place = Place(dp_bits)
     section, dp = place.section, place.dp
@@ -462,7 +463,7 @@
 
     def fetch(b, k):
         src = (x_hbm, e_hbm, g_hbm)[k]
-        dst = (R.xv, R.ev, R.gv)[k]
+        dst = (R.grS.at[0], R.stS.at[0], R.grS.at[1])[k]
         start = pl.multiple_of(b * CH, CH)
         return pltpu.make_async_copy(
             src.at[pl.ds(pl.multiple_of(section * rows, CH) + start, CH), :],
@@ -486,8 +487,8 @@
         total = jnp.sum(kept.astype(F32), axis=1, keepdims=True).astype(jnp.int32)
         R.used_v[p:p + 1, :] = jnp.broadcast_to(total, (1, 128))
 
-    k_iota = lax.broadcasted_iota(jnp.int32, (KEYS, SLOTS), 0)
-    q_iota = lax.broadcasted_iota(jnp.int32, (KEYS, SLOTS), 1)
+    k_iota = lax.broadcasted_iota(jnp.int32, (USED, SLOTS), 0)
+    q_iota = lax.broadcasted_iota(jnp.int32, (USED, SLOTS), 1)
 
     def out_copies(b, k):
         stage, out = ((R.stS, st_hbm), (R.grS, gr_hbm))[k]
@@ -531,10 +532,10 @@
                 fetch(b, k).wait()
             tok = slice(c * CH, c * CH + CH)
             src = pl.ds(pl.multiple_of(b * CH, CH), CH)
-            e = R.ev[src, :].T
+            e = R.stS[0, src, :].T
             R.eT[:, tok] = e
-            R.uT[:, tok] = R.xv[src, :].T.astype(F32) + e.astype(F32)
-            grad = R.gv[src, :].T
+            R.uT[:, tok] = R.grS[0, src, :].T.astype(F32) + e.astype(F32)
+            grad = R.grS[1, src, :].T
             R.gT[:, tok] = grad.astype(F32)
             R.lowT[1, :, tok] = grad
         R.load = load
@@ -624,15 +625,15 @@
         out_specs=[hbm, hbm, vmem, vmem],
         scratch_shapes=[pltpu.VMEM(s, t) for s, t in SCRATCH.values()] + list(comm_scratch(rows, rest).values()),
         compiler_params=pltpu.CompilerParams(
-            vmem_limit_bytes=62 * 1024 * 1024, collective_id=0, has_side_effects=True),
+            vmem_limit_bytes=57 * 1024 * 1024, collective_id=0, has_side_effects=True),
     )(x, e, g, counts, lengths, *params)
 
 
-CHUNKS = 8
+CHUNKS = 2
 
 
 def widen_kernel(st_ref, gr_ref, sums_ref, vec_ref, st_out, gr_out, n1g, n1b, wq, qb, wk, wv, vb, wo, ob, n2g, n2b, wu, ub, wd, db,
-                 st_v, gr_v, gr_w, sums_v, wd_v, wu_v, wa_v, st_in, gr_in, sum_in, st_sem, gr_sem, w_sem):
+                 st_v, gr_v, gr_w, sums_v, wd_v, wu_v, wa_v, st_in, gr_in, sum_in, st_sem, gr_sem, w_sem, v_sem, ub_v, *vec_v):
     block = st_v.shape[0] // CHUNKS
     sums_in = [pltpu.make_async_copy(sums_ref.at[rows, :], sums_v.at[rows, :], sum_in.at[i])
                for i, rows in enumerate((pl.ds(0, FF), pl.ds(FF, FF + D + QKV_ROWS)))]
@@ -654,8 +655,13 @@
         gr_w[parts[i], :] = gr_v[parts[i], :].astype(F32)
         out(gr_w.at[parts[i], :], gr_out.at[0, parts[i], :], gr_sem.at[i])
 
+    for j in range(FF // D):
+        ub_v[D * j:D * j + D] = vec_ref[8 + j]
+    out(ub_v, ub, v_sem.at[8])
+    for j, (r, v) in enumerate(zip((n1g, n1b, qb, vb, ob, n2g, n2b, db), vec_v)):
+        v[...] = vec_ref[j]
+        out(v, r, v_sem.at[j])
     gradients(0)
-    gradients(1)
     sums_in[0].wait()
     wd_v[...] = sums_v[0:FF, :].astype(F32)
     out(wd_v, wd, w_sem.at[0])
@@ -666,12 +672,8 @@
     wa_v[...] = sums_v[2 * FF:2 * FF + 4 * D, :].astype(F32)
     for j, r in enumerate((wo, wq, wk, wv)):
         out(wa_v.at[D * j:D * j + D, :], r, w_sem.at[2 + j])
-    for i in range(2, CHUNKS):
+    for i in range(1, CHUNKS):
         gradients(i)
-    for j in range(FF // D):
-        ub[D * j:D * j + D] = vec_ref[8 + j]
-    for j, r in enumerate((n1g, n1b, qb, vb, ob, n2g, n2b, db)):
-        r[...] = vec_ref[j]
     for i in range(CHUNKS):
         st_ins[i].wait()
         out(st_v.at[parts[i], :], st_out.at[0, parts[i], :], st_sem.at[i])
@@ -690,12 +692,12 @@
         widen_kernel,
         out_shape=outs,
         in_specs=[hbm, hbm, hbm, vmem],
-        out_specs=[hbm, hbm] + [hbm if len(p.shape) == 2 else vmem for p in params],
+        out_specs=[hbm] * len(outs),
         scratch_shapes=[
             pltpu.VMEM((local, 256), BF), pltpu.VMEM((local, 256), BF), pltpu.VMEM((local, 256), F32),
             pltpu.VMEM(sums.shape, BF), pltpu.VMEM((FF, D), F32), pltpu.VMEM((D, FF), F32), pltpu.VMEM((4 * D, D), F32),
-            dma((CHUNKS,)), dma((CHUNKS,)), dma((2,)), dma((CHUNKS,)), dma((CHUNKS,)), dma((6,))],
-        compiler_params=pltpu.CompilerParams(vmem_limit_bytes=60 * 1024 * 1024),
+            dma((CHUNKS,)), dma((CHUNKS,)), dma((2,)), dma((CHUNKS,)), dma((CHUNKS,)), dma((6,)), dma((9,)), pltpu.VMEM((FF,), F32)] + [pltpu.VMEM((D,), F32)] * 8,
+        compiler_params=pltpu.CompilerParams(vmem_limit_bytes=58 * 1024 * 1024),
     )(st, gr, sums, vec)
 
 

time: 103 us -> 101 us (0.981)
  Pallas kernels: 103 us -> 100 us
    pallas_call x1, Pallas kernels: 7.54 us -> 6.03 us  [widen(): pl.pallas_call(widen_kernel, out_shape=outs, in_specs=[hbm, hbm, hbm, vme...]
where the time goes in v6:
time: 101 us
  Pallas kernels  100 us (99%)
    pallas_call x1, Pallas kernels, compute(): pl.pallas_call(functools.partial(kernel, dp_bits), out_shape=outs, in_spe...  94.4 us
    pallas_call x1, Pallas kernels, widen(): pl.pallas_call(widen_kernel, out_shape=outs, in_specs=[hbm, hbm, hbm, vme...  6.03 us

profile of v6, /device:TPU:0, one launch (start us, length us, event | category | flops | bytes accessed | tf_op | source)
XLA Modules:
  0.0 101.1 jit_solution(5718971302296060563)
XLA Ops:
  0.7 94.4 %shard_map.323 = (bf16[4096,256]{1,0:T(8,128)(2,1)}, bf16[4096,256]{1,0:T(8,128)(2,1)}, bf16[3072,256]{1,0:T(8,128)(2,1)}, f32[16,256]{1,0:T(8,128)}) custom-call(bf16[4096,256]{1,0:T(8,128)(2,1)} %x_hbm.1, bf16[4096,256]{1,0:T(8,128)(2,1)} %e_hbm.1, bf16[4096,256]{1,0:T(8,128)(2,1)} %g_hbm.1, s32[32]{0:T(128)} %counts_ref.1, s32[32,50]{1,0:T(8,128)} %lengths_ref.1, ...), custom_call_target="tpu_custom_call" | custom-call | tf_op jit(solution)/shard_map/pallas_call | solution.py:621
  95.0 6.0 %shard_map.324 = (bf16[1,4096,256]{2,1,0:T(8,128)(2,1)}, f32[1,4096,256]{2,1,0:T(8,128)}, f32[256]{0:T(256)}, f32[256]{0:T(256)}, f32[256,256]{1,0:T(8,128)}, /*...) custom-call(bf16[4096,256]{1,0:T(8,128)(2,1)} %get-tuple-element.21., ...), custom_call_target="tpu_custom_call" | custom-call | tf_op jit(solution)/shard_map/pallas_call | solution.py:691

commit v7 on v6

--- a/solution.py
+++ b/solution.py
@@ -286,6 +286,7 @@
 MESH = pl.DeviceIdType.MESH
 CUBE = (("dp", 2), ("section", 1), ("dp", 4))
 PEERS = 7
+FARTHEST_FIRST = (7, 6, 5, 3, 4, 2, 1)
 
 
 class Place:
@@ -351,7 +352,7 @@
         c.wait_recv()
         small = pl.ds(self.cbuf, n)
         waits = []
-        for m in range(1, PEERS + 1):
+        for m in FARTHEST_FIRST:
             device, number = place.peer(m)
             at = pl.multiple_of(number * n, 16)
             R.cube_send[m - 1, small, :] = (R.acc[pl.ds(pl.multiple_of(self.keep + at, 16), n), :]
@@ -374,7 +375,7 @@
         own = pl.ds(self.own, n)
         R.sums[own, :] = total.astype(BF)
         waits = []
-        for m in range(1, PEERS + 1):
+        for m in FARTHEST_FIRST:
             waits.append(self.copy(R.sums.at[own, :], R.sums.at[own, :], PEERS + m, place.peer(m)[0]))
         yield
         for c in waits:
@@ -402,7 +403,7 @@
         c.wait_recv()
         R.vec_cube[place.cube] = R.vec_send[0] + R.vec_recv[0]
         waits = []
-        for m in range(1, PEERS + 1):
+        for m in FARTHEST_FIRST:
             waits.append(self.copy(R.vec_cube.at[place.cube], R.vec_cube.at[place.cube], m, place.peer(m)[0]))
         yield
         for c in waits:

time: 101 us -> 102 us (level)
  no operation moved by 1% of the time
where the time goes in v7:
time: 102 us; the launch traced here: 101 us
  Pallas kernels  101 us (99%)
    pallas_call x1, Pallas kernels, compute(): pl.pallas_call(functools.partial(kernel, dp_bits), out_shape=outs, in_spe...  94.6 us
    pallas_call x1, Pallas kernels, widen(): pl.pallas_call(widen_kernel, out_shape=outs, in_specs=[hbm, hbm, hbm, vme...  6.03 us

profile of v7, /device:TPU:0, one launch (start us, length us, event | category | flops | bytes accessed | tf_op | source)
XLA Modules:
  0.0 101.3 jit_solution(7977821410367971376)
XLA Ops:
  0.7 94.6 %shard_map.323 = (bf16[4096,256]{1,0:T(8,128)(2,1)}, bf16[4096,256]{1,0:T(8,128)(2,1)}, bf16[3072,256]{1,0:T(8,128)(2,1)}, f32[16,256]{1,0:T(8,128)}) custom-call(bf16[4096,256]{1,0:T(8,128)(2,1)} %x_hbm.1, bf16[4096,256]{1,0:T(8,128)(2,1)} %e_hbm.1, bf16[4096,256]{1,0:T(8,128)(2,1)} %g_hbm.1, s32[32]{0:T(128)} %counts_ref.1, s32[32,50]{1,0:T(8,128)} %lengths_ref.1, ...), custom_call_target="tpu_custom_call" | custom-call | tf_op jit(solution)/shard_map/pallas_call | solution.py:622
  95.2 6.0 %shard_map.324 = (bf16[1,4096,256]{2,1,0:T(8,128)(2,1)}, f32[1,4096,256]{2,1,0:T(8,128)}, f32[256]{0:T(256)}, f32[256]{0:T(256)}, f32[256,256]{1,0:T(8,128)}, /*...) custom-call(bf16[4096,256]{1,0:T(8,128)(2,1)} %get-tuple-element.21., ...), custom_call_target="tpu_custom_call" | custom-call | tf_op jit(solution)/shard_map/pallas_call | solution.py:692
